TPU v7x, 128 devices: a whole 4x4x4 slice. The times are simulated.
128 devices in a mesh: ctx: 32 (over z, y_lo, x), tp: 4 (over y_hi, core).
Axes of the slice: x: 4, y: 4 (y_hi: 2, y_lo: 2; y = y_hi * 2 + y_lo), z: 4, core: 2. Of those that a mesh axis runs over, the one named last changes fastest.
Arguments:
- q_nope: bfloat16 [4096, 64, 128], P('ctx', 'tp'), may hold values from -6 to 6
- q_rope: bfloat16 [4096, 64, 64], P('ctx', 'tp'), may hold values from -16 to 16
- latent: bfloat16 [4096, 576], P('ctx'), may hold values from -6 to 6
- up_keys: bfloat16 [64, 128, 512], P('tp'), may hold values from -0.25 to 0.25
- up_values: bfloat16 [64, 512, 128], P('tp'), may hold values from -1.5 to 1.5
- out_grad: bfloat16 [4096, 64, 128], P('ctx', 'tp'), may hold values from -6 to 6
Outputs:
- attn_out: bfloat16 [4096, 64, 128], P('ctx', 'tp')
- grad_q_nope: bfloat16 [4096, 64, 128], P('ctx', 'tp')
- grad_q_rope: bfloat16 [4096, 64, 64], P('ctx', 'tp')
- grad_latent: float32 [4096, 576], P('ctx')
All inputs are finite; a program needn't handle non-finite values.
Results may differ from a plain program's by a relative error of at most 0.034.
Values may be sent and summed in bfloat16 or wider, within the bound.
A program may use at most 192 MiB of HBM per device.

v0:
```python
import jax
import jax.numpy as jnp
from jax import lax
from jax.sharding import PartitionSpec as P


def tile_scores(queries, key_rows, scale_factor):
    return (
        jnp.einsum("qhc,kc->hqk", queries, key_rows, preferred_element_type=jnp.float32)
        * scale_factor
    )


def merge_scores(top_now, total_now, scores):
    top_new = jnp.maximum(top_now, jnp.max(scores, axis=2))
    total_new = total_now * jnp.exp(top_now - top_new) + jnp.sum(
        jnp.exp(scores - top_new[:, :, None]), axis=2
    )
    return (top_new, total_new)


def backward_tile(tile, queries, grads, row_delta, key_rows, lat_width, scale_factor):
    low_tile = tile.astype(jnp.bfloat16)
    dprobs = jnp.einsum(
        "qhc,kc->hqk", grads, key_rows[:, :lat_width], preferred_element_type=jnp.float32
    )
    grad_tile = (tile * (dprobs - row_delta[:, :, None]) * scale_factor).astype(jnp.bfloat16)
    grad_part = jnp.einsum("hqk,kc->qhc", grad_tile, key_rows, preferred_element_type=jnp.float32)
    latent_term = jnp.einsum("hqk,qhc->kc", grad_tile, queries, preferred_element_type=jnp.float32)
    value_term = jnp.einsum("hqk,qhc->kc", low_tile, grads, preferred_element_type=jnp.float32)
    pad_width = key_rows.shape[1] - lat_width
    return (grad_part, latent_term + jnp.pad(value_term, ((0, 0), (0, pad_width))))


def body(q_nope, q_rope, latent, up_keys, up_values, out_grad):
    row_count = q_nope.shape[0]
    head_count = q_nope.shape[1]
    half_rows = row_count // 2
    lat_width = up_keys.shape[2]
    full_width = latent.shape[1]
    cycle_size = lax.axis_size("ctx")
    myself = lax.axis_index("ctx")
    scale_factor = (q_nope.shape[2] + q_rope.shape[2]) ** (-0.5)
    projected = jnp.einsum("shd,hdc->shc", q_nope, up_keys, preferred_element_type=jnp.float32)
    absorbed = jnp.concatenate([projected.astype(jnp.bfloat16), q_rope], axis=2)
    triangle = jnp.tril(jnp.ones((row_count, row_count), dtype=bool))

    def pick_branch(source):
        return jnp.where(source < myself, 0, jnp.where(source > myself, 1, 2))

    def first_fold(carried, shards):
        shard_count = shards.shape[0] // row_count

        def first_one_shard(shard_num, state_now):
            key_rows = lax.dynamic_slice_in_dim(shards, shard_num * row_count, row_count, 0)
            source = shard_num

            def first_earlier(state_in):
                top_now, total_now, stored, diagonal = state_in
                scores = tile_scores(absorbed, key_rows[:half_rows], scale_factor)
                top_new, total_new = merge_scores(top_now, total_now, scores)
                stored = lax.dynamic_update_index_in_dim(
                    stored, scores.reshape(head_count, -1), source, 0
                )
                return (top_new, total_new, stored, diagonal)

            def first_later(state_in):
                top_now, total_now, stored, diagonal = state_in
                scores = tile_scores(absorbed[half_rows:], key_rows, scale_factor)
                top_late, total_late = merge_scores(
                    top_now[:, half_rows:], total_now[:, half_rows:], scores
                )
                top_now = top_now.at[:, half_rows:].set(top_late)
                total_now = total_now.at[:, half_rows:].set(total_late)
                stored = lax.dynamic_update_index_in_dim(
                    stored, scores.reshape(head_count, -1), source, 0
                )
                return (top_now, total_now, stored, diagonal)

            def first_own_rows(state_in):
                top_now, total_now, stored, diagonal = state_in
                scores = jnp.where(
                    triangle[None], tile_scores(absorbed, key_rows, scale_factor), -jnp.inf
                )
                top_new, total_new = merge_scores(top_now, total_now, scores)
                return (top_new, total_new, stored, scores)

            return lax.switch(
                pick_branch(source), [first_earlier, first_later, first_own_rows], state_now
            )

        return lax.fori_loop(0, shard_count, first_one_shard, carried)

    start_state = (
        jnp.full((head_count, row_count), -jnp.inf, jnp.float32),
        jnp.zeros((head_count, row_count), jnp.float32),
        jnp.zeros((cycle_size, head_count, row_count * half_rows), jnp.float32),
        jnp.zeros((head_count, row_count, row_count), jnp.float32),
    )
    top_all, total_all, stored, diagonal = first_fold(
        start_state, lax.all_gather(latent, "ctx", axis=0, tiled=True)
    )
    log_total = top_all + jnp.log(total_all)

    def second_fold(carried, shards):
        shard_count = shards.shape[0] // row_count

        def second_one_shard(shard_num, accum):
            key_rows = lax.dynamic_slice_in_dim(shards, shard_num * row_count, row_count, 0)
            saved = lax.dynamic_index_in_dim(stored, shard_num, 0, keepdims=False)

            def second_earlier(accum_in):
                tile = jnp.exp(
                    saved.reshape(head_count, row_count, half_rows) - log_total[:, :, None]
                ).astype(jnp.bfloat16)
                return accum_in + jnp.einsum(
                    "hqk,kc->qhc",
                    tile,
                    key_rows[:half_rows, :lat_width],
                    preferred_element_type=jnp.float32,
                )

            def second_later(accum_in):
                tile = jnp.exp(
                    saved.reshape(head_count, half_rows, row_count) - log_total[:, half_rows:, None]
                ).astype(jnp.bfloat16)
                return accum_in.at[half_rows:].add(
                    jnp.einsum(
                        "hqk,kc->qhc",
                        tile,
                        key_rows[:, :lat_width],
                        preferred_element_type=jnp.float32,
                    )
                )

            def second_own_rows(accum_in):
                tile = jnp.exp(diagonal - log_total[:, :, None]).astype(jnp.bfloat16)
                return accum_in + jnp.einsum(
                    "hqk,kc->qhc", tile, key_rows[:, :lat_width], preferred_element_type=jnp.float32
                )

            return lax.switch(
                pick_branch(shard_num), [second_earlier, second_later, second_own_rows], accum
            )

        return lax.fori_loop(0, shard_count, second_one_shard, carried)

    latent_out = second_fold(
        jnp.zeros((row_count, head_count, lat_width), jnp.float32),
        lax.all_gather(latent, "ctx", axis=0, tiled=True),
    )
    latent_low = latent_out.astype(jnp.bfloat16)
    attn_out = jnp.einsum(
        "qhc,hcv->qhv", latent_low, up_values, preferred_element_type=jnp.float32
    ).astype(jnp.bfloat16)
    grad_lat_out = jnp.einsum(
        "qhv,hcv->qhc", out_grad, up_values, preferred_element_type=jnp.float32
    ).astype(jnp.bfloat16)
    row_delta = jnp.sum(grad_lat_out.astype(jnp.float32) * latent_out, axis=2).T

    def third_fold(carried, shards):
        shard_count = shards.shape[0] // row_count

        def third_one_shard(shard_num, state_now):
            key_rows = lax.dynamic_slice_in_dim(shards, shard_num * row_count, row_count, 0)
            source = shard_num
            saved = lax.dynamic_index_in_dim(stored, source, 0, keepdims=False)

            def third_earlier(state_in):
                grad_acc, latent_terms = state_in
                tile = jnp.exp(
                    saved.reshape(head_count, row_count, half_rows) - log_total[:, :, None]
                )
                grad_part, latent_term = backward_tile(
                    tile,
                    absorbed,
                    grad_lat_out,
                    row_delta,
                    key_rows[:half_rows],
                    lat_width,
                    scale_factor,
                )
                latent_term = jnp.concatenate(
                    [latent_term, jnp.zeros((half_rows, full_width), jnp.float32)], axis=0
                )
                return (
                    grad_acc + grad_part,
                    lax.dynamic_update_index_in_dim(latent_terms, latent_term, source, 0),
                )

            def third_later(state_in):
                grad_acc, latent_terms = state_in
                tile = jnp.exp(
                    saved.reshape(head_count, half_rows, row_count) - log_total[:, half_rows:, None]
                )
                grad_part, latent_term = backward_tile(
                    tile,
                    absorbed[half_rows:],
                    grad_lat_out[half_rows:],
                    row_delta[:, half_rows:],
                    key_rows,
                    lat_width,
                    scale_factor,
                )
                return (
                    grad_acc.at[half_rows:].add(grad_part),
                    lax.dynamic_update_index_in_dim(latent_terms, latent_term, source, 0),
                )

            def third_own_rows(state_in):
                grad_acc, latent_terms = state_in
                tile = jnp.exp(diagonal - log_total[:, :, None])
                grad_part, latent_term = backward_tile(
                    tile, absorbed, grad_lat_out, row_delta, key_rows, lat_width, scale_factor
                )
                return (
                    grad_acc + grad_part,
                    lax.dynamic_update_index_in_dim(latent_terms, latent_term, source, 0),
                )

            return lax.switch(
                pick_branch(source), [third_earlier, third_later, third_own_rows], state_now
            )

        return lax.fori_loop(0, shard_count, third_one_shard, carried)

    grad_start = (
        jnp.zeros((row_count, head_count, full_width), jnp.float32),
        jnp.zeros((cycle_size, row_count, full_width), jnp.float32),
    )
    grad_acc, latent_terms = third_fold(
        grad_start, lax.all_gather(latent, "ctx", axis=0, tiled=True)
    )
    grad_absorbed = grad_acc.astype(jnp.bfloat16)
    grad_q_nope = jnp.einsum(
        "qhc,hdc->qhd", grad_absorbed[:, :, :lat_width], up_keys, preferred_element_type=jnp.float32
    ).astype(jnp.bfloat16)
    grad_q_rope = grad_absorbed[:, :, lat_width:]
    flat_terms = latent_terms.reshape(cycle_size * row_count, full_width)
    context_sum = lax.psum_scatter(
        flat_terms.astype(jnp.bfloat16), "ctx", scatter_dimension=0, tiled=True
    )
    grad_latent = lax.psum(context_sum, "tp").astype(jnp.float32)
    return (attn_out, grad_q_nope, grad_q_rope, grad_latent)


def solution(mesh):
    placed = (
        P("ctx", "tp", None),
        P("ctx", "tp", None),
        P("ctx", None),
        P("tp", None, None),
        P("tp", None, None),
        P("ctx", "tp", None),
    )
    return jax.shard_map(
        body,
        mesh=mesh,
        in_specs=placed,
        out_specs=(
            P("ctx", "tp", None),
            P("ctx", "tp", None),
            P("ctx", "tp", None),
            P("ctx", None),
        ),
        check_vma=False,
    )
```

profile of v0, /device:TPU:1, one launch (start us, length us, event | category | flops | bytes accessed | tf_op | source)
XLA Modules:
  0.0 1925.7 jit_solution(3031664182203646174)
XLA Ops:
  16.4 118.6 %all-gather.2.cloned.1.call-done = bf16[4096,576]{0,1:T(8,128)(2,1)} async-done(((bf16[128,576]{0,1:T(8,128)(2,1)}), bf16[4096,576]{0,1:T(8,128)(2,1)}) %all-gather.2.cloned.1.call-update) | async-done | bytes 4718608 | tf_op jit(solution)/shard_map/all_gather | solution.py:150
  135.0 7.8 broadcast_in_dim.69
  143.9 198.3 %while.54 = (s32[]{:T(128)}, f32[16,128]{1,0:T(8,128)S(1)}, f32[16,128]{1,0:T(8,128)S(1)}, f32[32,16,8192]{2,1,0:T(8,128)}, f32[16,128,128]{2,1,0:T(8,128)}, /*i...) while((s32[]{:T(128)}, f32[16,128]{1,0:T(8,128)S(1)}, ...), condition=%wide.region_10.11_spmd.clone, body=%wide.region_0.10_spmd.clone.sunk | while | flops 303321088 | bytes 7463385 | solution.py:92
  144.9 6.3 conditional.9
  342.2 7.6 copy.99
  352.4 186.2 %while.52 = (s32[]{:T(128)}, f32[128,16,512]{2,0,1:T(8,128)}, s32[]{:T(128)}, bf16[4096,576]{1,0:T(8,128)(2,1)}, f32[32,16,8192]{2,1,0:T(8,128)}, /*index=5*/f32...) while((s32[]{:T(128)}, f32[128,16,512]{2,0,1:T(8,128)}, ...), condition=%wide.region_15.16_spmd, body=%wide.region_11.0_spmd.sunk | while | flops 270008320 | bytes 11903361 | solution.py:146
  353.3 5.3 conditional.7
  353.3 5.2 bitcast_add_fusion.2
  359.5 4.9 conditional.7
  371.1 4.9 conditional.7
  376.9 4.9 conditional.7
  400.2 4.9 conditional.7
  406.0 4.9 conditional.7
  417.6 4.9 conditional.7
  429.2 4.9 conditional.7
  446.6 4.9 conditional.7
  458.2 4.9 conditional.7
  464.1 4.9 conditional.7
  475.7 4.9 conditional.7
  487.3 4.9 conditional.7
  504.7 4.9 conditional.7
  516.3 4.9 conditional.7
  522.1 4.9 conditional.7
  533.7 4.9 conditional.7
  538.6 5.5 copy.101
  558.4 336.3 %while.53 = (s32[]{:T(128)}, f32[128,16,576]{2,0,1:T(8,128)}, bf16[32,128,576]{1,2,0:T(8,128)(2,1)}, s32[]{:T(128)}, f32[32,16,8192]{2,1,0:T(8,128)}, /*index=5*...) while((s32[]{:T(128)}, f32[128,16,576]{2,0,1:T(8,128)}, ...), condition=%wide.region_21.22_spmd, body=%wide.region_17.21_spmd.sunk | while | flops 1143939072 | bytes 65118848 | solution.py:225
  560.4 23.9 %conditional.8 = (f32[128,16,576]{2,0,1:T(8,128)}, bf16[32,128,576]{1,2,0:T(8,128)(2,1)}) conditional(s32[]{:T(128)} %clamp.26, (f32[16,8192]{1,0:T(8,128)S(1)}, f32[16,128]{1,0:T(8,128)S(1)}, bf16[128,576]{1,0:T(8,128)(2,1)S(1)}, bf16[128,16,512]{2,0,1:T(8,128)(2,1)}, f32[16,128]{1,0:T(8,128)S(1)}, ...), branch_computations={%region_18.18_spmd, %region_19.19_spmd, %region_20.20_spmd} | conditional | flops 1143939072 | bytes 63774884 | solution.py:221
  567.4 5.8 copy.91
  573.2 5.3 bitcast_add_fusion.5
  578.5 5.8 copy.87
  586.3 8.0 conditional.8
  596.3 8.0 conditional.8
  606.4 8.0 conditional.8
  616.4 8.0 conditional.8
  626.4 8.0 conditional.8
  636.4 8.0 conditional.8
  646.4 8.0 conditional.8
  656.4 8.0 conditional.8
  666.4 8.0 conditional.8
  676.4 8.0 conditional.8
  686.4 8.0 conditional.8
  696.5 8.0 conditional.8
  706.5 8.0 conditional.8
  716.5 8.0 conditional.8
  726.5 8.0 conditional.8
  736.5 8.0 conditional.8
  746.5 8.0 conditional.8
  756.5 8.0 conditional.8
  766.5 8.0 conditional.8
  776.6 8.0 conditional.8
  786.6 8.0 conditional.8
  796.6 8.0 conditional.8
  806.6 8.0 conditional.8
  816.6 8.0 conditional.8
  826.6 8.0 conditional.8
  836.6 8.0 conditional.8
  846.6 8.0 conditional.8
  856.6 8.0 conditional.8
  866.7 8.0 conditional.8
  876.7 8.0 conditional.8
  886.7 8.0 conditional.8
  894.7 7.6 copy.127
  907.9 948.5 %reduce-scatter.4.cloned.1.call-done = bf16[128,576]{1,0:T(8,128)(2,1)} async-done(((bf16[4096,576]{1,0:T(8,128)(2,1)}), bf16[128,576]{1,0:T(8,128)(2,1)}) %reduce-scatter.4.cloned.1.call-update) | async-done | bytes 147472
  1864.2 53.4 %all-reduce.6.cloned.1.call-done = bf16[128,576]{0,1:T(8,128)(2,1)} async-done(((bf16[128,576]{0,1:T(8,128)(2,1)}), bf16[128,576]{0,1:T(8,128)(2,1)}) %all-reduce.6.cloned.1.call-update) | async-done | bytes 147472 | tf_op jit(solution)/shard_map/psum | solution.py:243
  (1130 shorter events, 944.5 us)
Async XLA Ops:
  7.2 536.9 %copy-start = (bf16[16,512,128]{2,1,0:T(8,128)(2,1)S(1)}, bf16[16,512,128]{2,1,0:T(8,128)(2,1)}, u32[]{:S(2)}) copy-start(bf16[16,512,128]{2,1,0:T(8,128)(2,1)} %param.33) | copy-start | bytes 6291460
  7.2 3.3 copy-start.10
  7.2 127.8 %all-gather.2.cloned.1.call-start = ((), (), s32[]{:S(2)}) async-start(), calls=%async_computation.1 | async-start | bytes 4866048 | tf_op jit(solution)/shard_map/all_gather | solution.py:150
  7.9 1848.4 %reduce-scatter.4.cloned.1.call-start = ((), (), s32[]{:S(2)}) async-start(), calls=%async_computation.3 | async-start | bytes 5406720
  538.6 5.5 copy-start.9
  562.0 2.6 copy-start.2
  562.0 3.6 copy-start.5
  564.6 2.8 copy-start.7
  567.4 5.8 copy-start.8
  586.4 2.4 copy-start.1
  586.4 2.9 copy-start.4
  596.4 2.9 copy-start.4
  606.4 2.4 copy-start.1
  606.4 2.9 copy-start.4
  616.4 2.4 copy-start.1
  616.4 2.9 copy-start.4
  626.4 2.4 copy-start.1
  626.4 2.9 copy-start.4
  636.4 2.4 copy-start.1
  636.4 2.9 copy-start.4
  646.4 2.9 copy-start.4
  656.5 2.4 copy-start.1
  656.5 2.9 copy-start.4
  666.5 2.4 copy-start.1
  666.5 2.9 copy-start.4
  676.5 2.4 copy-start.1
  676.5 2.9 copy-start.4
  686.5 2.4 copy-start.1
  686.5 2.9 copy-start.4
  696.5 2.4 copy-start.1
  696.5 2.9 copy-start.4
  706.5 2.4 copy-start.1
  706.5 2.9 copy-start.4
  716.5 2.4 copy-start.1
  716.5 2.9 copy-start.4
  726.5 2.9 copy-start.4
  736.5 2.4 copy-start.1
  736.5 2.9 copy-start.4
  746.5 2.4 copy-start.1
  746.6 2.9 copy-start.4
  756.6 2.9 copy-start.4
  766.6 2.4 copy-start.1
  766.6 2.9 copy-start.4
  776.6 2.4 copy-start.1
  776.6 2.9 copy-start.4
  786.6 2.4 copy-start.1
  786.6 2.9 copy-start.4
  796.6 2.9 copy-start.4
  806.6 2.4 copy-start.1
  806.6 2.9 copy-start.4
  816.6 2.4 copy-start.1
  816.6 2.9 copy-start.4
  826.6 2.4 copy-start.1
  826.7 2.9 copy-start.4
  836.7 2.9 copy-start.4
  846.7 2.4 copy-start.1
  846.7 2.9 copy-start.4
  856.7 2.9 copy-start.4
  866.7 2.9 copy-start.4
  876.7 2.9 copy-start.4
  886.7 2.9 copy-start.4
  902.3 1015.2 %all-reduce.6.cloned.1.call-start = ((), (), s32[]{:S(2)}) async-start(), calls=%async_computation.2 | async-start | bytes 294912 | tf_op jit(solution)/shard_map/psum | solution.py:243
  902.6 4.6 copy-start.6
  907.9 954.3 %slice-start = ((bf16[128,16,576]{2,0,1:T(8,128)(2,1)}), bf16[128,16,64]{2,0,1:T(8,128)(2,1)S(1)}, s32[]{:S(2)}) async-start(bf16[128,16,576]{2,0,1:T(8,128)(2,1)} %convert_element_type.84), calls=%async_computation.4 | async-start | bytes 1048576 | tf_op jit(solution)/shard_map/slice | solution.py:238
  (10 other events, 24.0 us)
Sparse Core Ops, SparseCore 0:
  9.6 125.3 all-gather.1
  902.4 953.8 reduce-scatter.3
  1859.4 58.0 all-reduce.5
where the time goes:
time: 1950 us; the launch traced here: 1930 us
  waiting for transfers between devices  1120 us (57%)
  matrix products  422 us (22%)
  local copies, waits for them, and re-layouts  320 us (16%)
  other arithmetic  40.3 us (2%)
    unnamed x4, waiting for transfers between devices  949 us
    dot_general x32, matrix products, backward_tile(): jnp.einsum('hqk,kc->qhc', grad_tile, key_rows, preferred_element_type=jnp...  120 us
    all_gather x1, waiting for transfers between devices, body(): lax.all_gather(latent, 'ctx', axis=0, tiled=True)  119 us
    dot_general x31, matrix products, second_later(): jnp.einsum('hqk,kc->qhc', tile, key_rows[:, :lat_width], preferred_elemen...  104 us
    dot_general x32, matrix products, tile_scores(): jnp.einsum('qhc,kc->hqk', queries, key_rows, preferred_element_type=jnp.f...  61.9 us
    dot_general x32, matrix products, backward_tile(): jnp.einsum('qhc,kc->hqk', grads, key_rows[:, :lat_width], preferred_eleme...  61.7 us
    cond x256, local copies, waits for them, and re-layouts  58.8 us
    psum x1, waiting for transfers between devices, body(): grad_latent = lax.psum(context_sum, 'tp').astype(jnp.float32)  53.4 us
  transfers between devices with their start and end apart: 3, of which 3 were waited for; matrix products, arithmetic and copies ran while one was open for 1% of the time, Pallas kernels for 0%

commit v1 on v0

v1 whole, which is shorter than its diff:
```python
import functools, math
import jax, jax.numpy as jnp
from jax import lax
from jax.experimental import pallas as pl
from jax.experimental.pallas import tpu as pltpu
F32, BF16 = jnp.float32, jnp.bfloat16
SCALE = 192 ** -0.5
NEG = -1e30

def dot(a, b):
    return jnp.dot(a, b, preferred_element_type=F32)

def dot_nt(a, b):
    return lax.dot_general(a, b, (((1,), (1,)), ((), ())), preferred_element_type=F32)

def core(t0, lat, q, qr, og, wk, wv, attn, gq, gqr, dl,
         A, AT, G, GT, LT, S, O, DA, m, l, lse, delta, dsb, pbb, acc):
    log2k = SCALE * math.log2(math.e)
    c_dyn = t0[0]
    tt = t0[1]
    @pl.loop(0, 8)
    def _(p):
        lanes = pl.ds(pl.multiple_of(p * 128, 128), 128)
        pa = dot(q[2 * p], wk[2 * p])
        pb = dot(q[2 * p + 1], wk[2 * p + 1])
        ga = dot_nt(og[2 * p], wv[2 * p])
        gb = dot_nt(og[2 * p + 1], wv[2 * p + 1])
        ra, rb = qr[2 * p], qr[2 * p + 1]
        for hf in range(2):
            r = slice(64 * hf, 64 * hf + 64)
            blk = jnp.concatenate([pa[r], pb[r]], axis=0)
            A[hf, lanes, :512] = blk.astype(BF16)
            AT[hf, :512, lanes] = blk.T.astype(BF16)
            rblk = jnp.concatenate([ra[r], rb[r]], axis=0)
            A[hf, lanes, 512:] = rblk
            AT[hf, 512:, lanes] = rblk.astype(F32).T.astype(BF16)
            gblk = jnp.concatenate([ga[r], gb[r]], axis=0)
            G[hf, lanes, :] = gblk.astype(BF16)
            GT[hf, :, lanes] = gblk.T.astype(BF16)
    m[...] = jnp.full_like(m, NEG)
    l[...] = jnp.zeros_like(l)
    O[...] = jnp.zeros_like(O)
    DA[...] = jnp.zeros_like(DA)
    c = c_dyn

    def fwd(t, hf):
        slot = jnp.where(hf == 1, t, 16 - t)
        base = jnp.where(hf == 1, 63 - c, c) * 64 - t * 256
        Lt = lat[pl.ds(pl.multiple_of(t * 256, 256), 256), :]
        diff = lax.broadcasted_iota(jnp.int32, (256, 256), 0) - lax.rem(lax.broadcasted_iota(jnp.int32, (256, 256), 1), 64)
        for ch in range(4):
            cs = slice(ch * 256, ch * 256 + 256)
            s = dot(Lt, AT[hf, :, cs]) * log2k
            S[slot, :, cs] = jnp.where(diff <= base, s, NEG)
        als = []
        for ch in range(4):
            cs = slice(ch * 256, ch * 256 + 256)
            s = S[slot, :, cs]
            mo = m[hf, :, cs]
            mn = jnp.maximum(mo, jnp.max(s, axis=0, keepdims=True))
            p = jnp.exp2(s - mn)
            al = jnp.exp2(mo - mn)
            m[hf, :, cs] = mn
            l[hf, :, cs] = l[hf, :, cs] * al + jnp.sum(p, axis=0, keepdims=True)
            pbb[:, cs] = p.astype(BF16)
            als.append(al)
        for ch in range(4):
            cs = slice(ch * 256, ch * 256 + 256)
            O[hf, :, cs] = O[hf, :, cs] * als[ch] + dot(LT[t, :512, :], pbb[:, cs])

    @pl.loop(0, 16)
    def _(t):
        LT[t] = lat[pl.ds(pl.multiple_of(t * 256, 256), 256), :].astype(F32).T.astype(BF16)
        @pl.when(t <= 15 - tt)
        def _():
            fwd(t, 1)
        @pl.when(t <= tt)
        def _():
            fwd(t, 0)
    for hf in range(2):
        for ch in range(4):
            cs = slice(ch * 256, ch * 256 + 256)
            lse[hf, :, cs] = m[hf, :, cs] + jnp.log2(l[hf, :, cs])
            o = O[hf, :, cs] * (1.0 / l[hf, :, cs])
            O[hf, :, cs] = o
            delta[hf, :, cs] = jnp.sum(GT[hf, :, cs].astype(F32) * o, axis=0, keepdims=True)

    def bwd(t, hf):
        slot = jnp.where(hf == 1, t, 16 - t)
        Lt = lat[pl.ds(pl.multiple_of(t * 256, 256), 256), :512]
        for ch in range(4):
            cs = slice(ch * 256, ch * 256 + 256)
            dp = dot(Lt, GT[hf, :, cs])
            p = jnp.exp2(S[slot, :, cs] - lse[hf, :, cs])
            ds = (p * (dp - delta[hf, :, cs]) * SCALE).astype(BF16)
            dsb[:, cs] = ds
            pbb[:, cs] = p.astype(BF16)
            DA[hf, :, cs] += dot(LT[t], ds)
        return dot(dsb[...], A[hf]), dot(pbb[...], G[hf])

    @pl.loop(0, 16)
    def _(t):
        rows = pl.ds(pl.multiple_of(t * 256, 256), 256)
        @pl.when(t <= 15 - tt)
        def _():
            a, b = bwd(t, 1)
            acc[:, :512] = a[:, :512] + b
            acc[:, 512:] = a[:, 512:]
        @pl.when(t > 15 - tt)
        def _():
            acc[...] = jnp.zeros((256, 576), F32)
        @pl.when(t <= tt)
        def _():
            a, b = bwd(t, 0)
            acc[:, :512] += a[:, :512] + b
            acc[:, 512:] += a[:, 512:]
        dl[rows, :] = acc[...].astype(BF16)
    @pl.loop(0, 8)
    def _(p):
        lanes = pl.ds(pl.multiple_of(p * 128, 128), 128)
        ob = [O[hf, :, lanes].T.astype(BF16) for hf in range(2)]
        db = [DA[hf, :, lanes].T.astype(BF16) for hf in range(2)]
        for e in range(2):
            r = slice(64 * e, 64 * e + 64)
            h = 2 * p + e
            o = jnp.concatenate([ob[0][r], ob[1][r]], axis=0)
            d = jnp.concatenate([db[0][r], db[1][r]], axis=0)
            attn[h] = dot(o, wv[h]).astype(BF16)
            gq[h] = dot_nt(d[:, :512], wk[h]).astype(BF16)
            gqr[h] = d[:, 512:]

SCR = [
    pltpu.VMEM((2, 1024, 576), BF16), pltpu.VMEM((2, 576, 1024), BF16),
    pltpu.VMEM((2, 1024, 512), BF16), pltpu.VMEM((2, 512, 1024), BF16),
    pltpu.VMEM((16, 576, 256), BF16), pltpu.VMEM((17, 256, 1024), F32),
    pltpu.VMEM((2, 512, 1024), F32), pltpu.VMEM((2, 576, 1024), F32),
    pltpu.VMEM((2, 1, 1024), F32), pltpu.VMEM((2, 1, 1024), F32), pltpu.VMEM((2, 1, 1024), F32), pltpu.VMEM((2, 1, 1024), F32),
    pltpu.VMEM((256, 1024), BF16), pltpu.VMEM((256, 1024), BF16), pltpu.VMEM((256, 576), F32),
]
def call():
    V = pl.BlockSpec(memory_space=pltpu.VMEM)
    return pl.pallas_call(core,
        out_shape=[jax.ShapeDtypeStruct((16, 128, 128), BF16), jax.ShapeDtypeStruct((16, 128, 128), BF16),
                   jax.ShapeDtypeStruct((16, 128, 64), BF16), jax.ShapeDtypeStruct((4096, 576), BF16)],
        in_specs=[pl.BlockSpec(memory_space=pltpu.SMEM)] + [V] * 6,
        out_specs=[V] * 4, scratch_shapes=SCR,
        compiler_params=pltpu.CompilerParams(vmem_limit_bytes=63 * 2**20))


def body(q_nope, q_rope, latent, up_keys, up_values, out_grad):
    c = lax.axis_index("ctx")
    info = jnp.stack([c, c // 4]).astype(jnp.int32)
    full = lax.all_gather(latent, "ctx", axis=0, tiled=True).reshape(32, 2, 64, 576)
    keys = jnp.concatenate([full[:, 0], full[::-1, 1]], axis=0).reshape(4096, 576)
    heads = lambda z: jnp.swapaxes(z, 0, 1)
    attn, gq, gqr, dl = call()(info, keys, heads(q_nope), heads(q_rope), heads(out_grad), up_keys, up_values)
    dl = dl.reshape(2, 32, 64, 576)
    dl = jnp.stack([dl[0], dl[1, ::-1]], axis=1).reshape(4096, 576)
    part = lax.psum_scatter(dl, "ctx", scatter_dimension=0, tiled=True)
    return heads(attn), heads(gq), heads(gqr), lax.psum(part, "tp").astype(F32)


def solution(mesh):
    from jax.sharding import PartitionSpec as P
    rows = P("ctx", "tp", None)
    return jax.shard_map(
        body, mesh=mesh,
        in_specs=(rows, rows, P("ctx", None), P("tp", None, None), P("tp", None, None), rows),
        out_specs=(rows, rows, rows, P("ctx", None)), check_vma=False)
```

time: 1950 us -> 470 us (0.24); the launches traced: 1930 us -> 470 us
  waiting for transfers between devices: 1120 us -> 368 us
  matrix products: 422 us -> 0 us
  local copies, waits for them, and re-layouts: 320 us -> 17.5 us
  Pallas kernels: 0 us -> 64 us
  other arithmetic: 40.3 us -> 6.58 us
    unnamed x4 -> x3, waiting for transfers between devices: 949 us -> 0.05 us
    dot_general x196 -> x0, matrix products: 422 us -> none  [the longest x32 120 us: backward_tile(): jnp.einsum('hqk,kc->qhc', grad_tile, key_rows, preferred_element_type=jnp...]
    reduce_scatter x0 -> x1, waiting for transfers between devices: none -> 168 us  [body(): part = lax.psum_scatter(dl, 'ctx', scatter_dimension=0, tiled=True)]
    dynamic_slice x96 -> x0, local copies, waits for them, and re-layouts: 88.9 us -> none  [the longest x32 29.8 us: second_one_shard(): lax.dynamic_slice_in_dim(shards, shard_num * row_count, row_count, 0)]
    pallas_call x0 -> x1, Pallas kernels: none -> 64 us  [body(): call()]
    cond x256 -> x0, local copies, waits for them, and re-layouts: 58.8 us -> none
    while x35 -> x0, local copies, waits for them, and re-layouts: 39.3 us -> none
    squeeze x32 -> x2, local copies, waits for them, and re-layouts: 34.6 us -> 3.22 us  [the longest x1 2.99 us: body(): full[:, 0]]
  transfers between devices with their start and end apart: 3 -> 3, of which waited for: 3 -> 3; matrix products, arithmetic and copies ran while one was open for 1% -> 2% of each run, Pallas kernels for 0% -> 0%
where the time goes in v1:
time: 470 us
  waiting for transfers between devices  368 us (78%)
  Pallas kernels  64 us (14%)
  local copies, waits for them, and re-layouts  17.5 us (4%)
  between operations  13.8 us (3%)
  other arithmetic  6.58 us (1%)
    reduce_scatter x1, waiting for transfers between devices, body(): part = lax.psum_scatter(dl, 'ctx', scatter_dimension=0, tiled=True)  168 us
    all_gather x1, waiting for transfers between devices, body(): lax.all_gather(latent, 'ctx', axis=0, tiled=True).reshape(32, 2, 64, 576)  141 us
    pallas_call x1, Pallas kernels, body(): call()  64 us
    psum x1, waiting for transfers between devices, body(): lax.psum(part, 'tp').astype(F32)  59 us
  transfers between devices with their start and end apart: 3, of which 3 were waited for; matrix products, arithmetic and copies ran while one was open for 2% of the time, Pallas kernels for 0%

profile of v1, /device:TPU:1, one launch (start us, length us, event | category | flops | bytes accessed | tf_op | source)
XLA Modules:
  0.0 469.9 jit_solution(15474870400936750506)
XLA Ops:
  7.2 0.0 all-gather.2.cloned.1.call-start
  7.2 1.7 copy.19
  8.9 0.0 all-gather.2.cloned.1.call-update
  8.9 0.0 reduce-scatter.2.cloned.1.call-start
  9.0 2.0 copy.22
  11.0 0.6 pad_add_fusion.t0
  11.5 2.4 copy_bitcast_fusion
  14.0 141.3 %all-gather.2.cloned.1.call-done = bf16[4096,576]{1,0:T(8,128)(2,1)} async-done(((bf16[128,576]{1,0:T(8,128)(2,1)}), bf16[4096,576]{1,0:T(8,128)(2,1)}) %all-gather.2.cloned.1.call-update) | async-done | bytes 4718608 | tf_op jit(solution)/shard_map/all_gather | solution.py:153
  155.3 3.0 slice_bitcast_fusion
  158.3 0.2 reverse_bitcast_fusion.1
  158.5 3.0 pad_maximum_fusion
  161.6 64.0 %shard_map.93 = (bf16[16,128,128]{2,1,0:T(8,128)(2,1)}, bf16[16,128,128]{2,1,0:T(8,128)(2,1)}, bf16[16,128,64]{2,1,0:T(8,128)(2,1)}, bf16[4096,576]{1,0:T(8,128)(2,1)}) custom-call(s32[2]{0:T(128)} %pad_add_fusion.t0, bf16[4096,576]{1,0:T(8,128)(2,1)} %bitcast.25, bf16[16,128,128]{2,1,0:T(8,128)(2,1)} %get-tuple-element.25.q, bf16[16,128,64]{2,1,0:T(8,128)(2,1)} %bitcast.30, ...), custom_call_target="tpu_custom_call" | custom-call | tf_op jit(solution)/shard_map/pallas_call | solution.py:156
  225.6 3.0 fusion
  228.5 0.2 reverse_bitcast_fusion
  228.8 3.0 pad_maximum_fusion.1
  231.8 0.0 copy-start.2
  231.8 0.0 copy-start.1
  231.8 0.0 copy-start
  231.8 0.0 reduce-scatter.2.cloned.1.call-update
  231.8 0.0 all-reduce.2.cloned.1.call-start
  231.9 167.5 %reduce-scatter.2.cloned.1.call-done = bf16[128,576]{1,0:T(8,128)(2,1)} async-done(((bf16[4096,576]{1,0:T(8,128)(2,1)}), bf16[128,576]{1,0:T(8,128)(2,1)}) %reduce-scatter.2.cloned.1.call-update) | async-done | bytes 147472 | tf_op jit(solution)/shard_map/reduce_scatter | solution.py:159
  399.4 0.0 all-reduce.2.cloned.1.call-update
  399.4 0.0 copy-done.2
  399.5 1.1 copy.25
  400.6 0.0 copy-done.1
  400.6 1.1 copy.26
  401.7 0.0 copy-done
  401.7 0.9 copy.27
  402.6 59.0 %all-reduce.2.cloned.1.call-done = bf16[128,576]{1,0:T(8,128)(2,1)} async-done(((bf16[128,576]{1,0:T(8,128)(2,1)}), bf16[128,576]{1,0:T(8,128)(2,1)}) %all-reduce.2.cloned.1.call-update) | async-done | bytes 147472 | tf_op jit(solution)/shard_map/psum | solution.py:160
  461.6 1.7 copy.28
Async XLA Ops:
  7.2 148.1 %all-gather.2.cloned.1.call-start = ((), (), s32[]{:S(2)}) async-start(), calls=%async_computation.1 | async-start | bytes 5406720 | tf_op jit(solution)/shard_map/all_gather | solution.py:153
  8.9 390.5 %reduce-scatter.2.cloned.1.call-start = ((), (), s32[]{:S(2)}) async-start(), calls=%async_computation.2 | async-start | bytes 5406720 | tf_op jit(solution)/shard_map/reduce_scatter | solution.py:159
  231.8 167.6 %copy-start.2 = (bf16[16,128,128]{2,1,0:T(8,128)(2,1)S(1)}, bf16[16,128,128]{2,1,0:T(8,128)(2,1)}, u32[]{:S(2)}) copy-start(bf16[16,128,128]{2,1,0:T(8,128)(2,1)} %get-tuple-element.8) | copy-start | bytes 1572868
  231.8 168.8 %copy-start.1 = (bf16[16,128,128]{2,1,0:T(8,128)(2,1)S(1)}, bf16[16,128,128]{2,1,0:T(8,128)(2,1)}, u32[]{:S(2)}) copy-start(bf16[16,128,128]{2,1,0:T(8,128)(2,1)} %get-tuple-element.9) | copy-start | bytes 1572868
  231.8 169.9 %copy-start = (bf16[16,128,64]{2,1,0:T(8,128)(2,1)S(1)}, bf16[16,128,64]{2,1,0:T(8,128)(2,1)}, u32[]{:S(2)}) copy-start(bf16[16,128,64]{2,1,0:T(8,128)(2,1)} %get-tuple-element.10) | copy-start | bytes 786436
  231.8 229.8 %all-reduce.2.cloned.1.call-start = ((), (), s32[]{:S(2)}) async-start(), calls=%async_computation.3 | async-start | bytes 327680 | tf_op jit(solution)/shard_map/psum | solution.py:160
Sparse Core Ops, SparseCore 0:
  10.2 145.0 all-gather.1
  231.9 167.4 reduce-scatter.1
  401.9 59.6 all-reduce.1

commit v2 on v1

v2 whole, which is shorter than its diff:
```python
import math

import jax
import jax.numpy as jnp
from jax import lax
from jax.experimental import pallas as pl
from jax.experimental.pallas import tpu as pltpu
from jax.sharding import PartitionSpec as P

F32, BF16 = jnp.float32, jnp.bfloat16
SCALE = 192**-0.5
LOG2_SCALE = SCALE * math.log2(math.e)
NEG = -1e30
MESH = pl.DeviceIdType.MESH


def dot(a, b):
    return jnp.dot(a, b, preferred_element_type=F32)


def dot_nt(a, b):
    return lax.dot_general(a, b, (((1,), (1,)), ((), ())), preferred_element_type=F32)


def remote(src, dst, send_sem, recv_sem, ctx, tp):
    return pltpu.make_async_remote_copy(
        src_ref=src, dst_ref=dst, send_sem=send_sem, recv_sem=recv_sem,
        device_id={"ctx": ctx, "tp": tp}, device_id_type=MESH,
    )


def kernel(lat, q, qr, og, wk, wv, attn, gq, gqr, gl,
           L, LT, A, AT, G, GT, S, O, DA, top, tot, lse, delta, dsb, pbb, acc,
           R1, R2, R3s, R3, fin,
           sx, rx, sz, rz, sy, ry, ss, rs, s1, r1, s2, r2, s3, r3, s4, r4):
    c, tp = lax.axis_index("ctx"), lax.axis_index("tp")
    z, yl, x = c // 8, (c // 4) % 2, c % 4
    yh, k = tp // 2, tp % 2
    t0 = c // 4
    sib = yh * 2 + 1 - k

    def cid(z_, yl_, x_):
        return z_ * 8 + yl_ * 4 + x_

    def tile_of(kind, line):
        return jnp.where(kind == 0, line, 15 - line)

    def block_at(x_):
        return pl.multiple_of(64 * jnp.where(k == 0, x_, 3 - x_), 64)

    def order(s):
        i = s % 4
        return i + jnp.where(i == 2, 1, 0) - jnp.where(i == 3, 1, 0), s // 4

    def line_at(dz, dy):
        return 2 * ((z + dz) % 4) + (yl + dy) % 2

    def active(kind, line):
        return (kind == 0) | (line >= t0)

    barrier = pltpu.get_barrier_semaphore()

    def hello(ctx, tp_):
        pl.semaphore_signal(barrier, inc=1, device_id={"ctx": ctx, "tp": tp_}, device_id_type=MESH)

    @pl.loop(1, 4)
    def _(i):
        hello(cid(z, yl, (x + i) % 4), tp)

    @pl.loop(1, 16)
    def _(i):
        hello(cid((z + i // 4) % 4, (yl + (i // 2) % 2) % 2, x), ((yh + i % 2) % 2) * 2 + k)

    hello(c, sib)
    hello(c, (1 - yh) * 2 + 1 - k)
    pl.semaphore_wait(barrier, 20)

    mine = tile_of(k, t0)

    def x_copy(dx):
        at = L.at[mine, pl.ds(block_at(x), 64), :]
        return remote(at, at, sx.at[dx - 1], rx.at[dx - 1], cid(z, yl, (x + dx) % 4), tp)

    def z_copy(dz):
        at = L.at[mine]
        return remote(at, at, sz.at[dz - 1], rz.at[3 - dz], cid((z + dz) % 4, yl, x), tp)

    def y_copy(dz, to):
        at = L.at[tile_of(k, line_at(dz, 0)), pl.ds(pl.multiple_of(128 * yh, 128), 128), :]
        return remote(at, at, sy.at[dz, to], ry.at[dz, yh], cid(z, 1 - yl, x), to * 2 + k)

    def core_copy(s, line):
        at = L.at[tile_of(k, line)]
        return remote(at, at, ss.at[s], rs.at[s], c, sib)

    L[mine, pl.ds(block_at(x), 64), :] = lat[pl.ds(pl.multiple_of(64 * k, 64), 64), :]
    for dx in (1, 3, 2):
        x_copy(dx).start()

    @pl.loop(0, 8)
    def _(p):
        cols = pl.ds(pl.multiple_of(p * 128, 128), 128)
        pa = dot(q[2 * p], wk[2 * p])
        pb = dot(q[2 * p + 1], wk[2 * p + 1])
        ga = dot_nt(og[2 * p], wv[2 * p])
        gb = dot_nt(og[2 * p + 1], wv[2 * p + 1])
        ra, rb = qr[2 * p], qr[2 * p + 1]
        for hf in range(2):
            r = slice(64 * hf, 64 * hf + 64)
            blk = jnp.concatenate([pa[r], pb[r]], axis=0)
            A[hf, cols, :512] = blk.astype(BF16)
            AT[hf, :512, cols] = blk.T.astype(BF16)
            rblk = jnp.concatenate([ra[r], rb[r]], axis=0)
            A[hf, cols, 512:] = rblk
            AT[hf, 512:, cols] = rblk.astype(F32).T.astype(BF16)
            gblk = jnp.concatenate([ga[r], gb[r]], axis=0)
            G[hf, cols, :] = gblk.astype(BF16)
            GT[hf, :, cols] = gblk.T.astype(BF16)

    top[...] = jnp.full_like(top, NEG)
    tot[...] = jnp.zeros_like(tot)
    O[...] = jnp.zeros_like(O)
    DA[...] = jnp.zeros_like(DA)

    def slot_of(t, hf):
        return jnp.where(hf == 1, t, 16 - t)

    def forward(t, hf):
        slot = slot_of(t, hf)
        base = jnp.where(hf == 1, 63 - c, c) * 64 - t * 256
        diff = lax.broadcasted_iota(jnp.int32, (256, 256), 0) - lax.rem(
            lax.broadcasted_iota(jnp.int32, (256, 256), 1), 64)
        for ch in range(4):
            cs = slice(ch * 256, ch * 256 + 256)
            s = dot(L[t], AT[hf, :, cs]) * LOG2_SCALE
            S[slot, :, cs] = jnp.where(diff <= base, s, NEG)
        shrink = []
        for ch in range(4):
            cs = slice(ch * 256, ch * 256 + 256)
            s = S[slot, :, cs]
            old = top[hf, :, cs]
            new = jnp.maximum(old, jnp.max(s, axis=0, keepdims=True))
            p = jnp.exp2(s - new)
            al = jnp.exp2(old - new)
            top[hf, :, cs] = new
            tot[hf, :, cs] = tot[hf, :, cs] * al + jnp.sum(p, axis=0, keepdims=True)
            pbb[:, cs] = p.astype(BF16)
            shrink.append(al)
        for ch in range(4):
            cs = slice(ch * 256, ch * 256 + 256)
            O[hf, :, cs] = O[hf, :, cs] * shrink[ch] + dot(LT[t, :512, :], pbb[:, cs])

    for dx in (1, 2, 3):
        x_copy(dx).wait_recv()
    for dz in (1, 3, 2):
        z_copy(dz).start()

    @pl.loop(0, 8)
    def _(s):
        dz, dy = order(s)
        line = line_at(dz, dy)

        @pl.when((dy == 0) & (dz > 0))
        def _():
            z_copy(4 - dz).wait_recv()

        @pl.when(dy == 0)
        def _():
            for to in range(2):
                y_copy(dz, to).start()

        @pl.when(dy == 1)
        def _():
            for frm in range(2):
                at = L.at[tile_of(k, line), 128 * frm:128 * frm + 128, :]
                remote(at, at, sy.at[dz, 0], ry.at[dz, frm], cid(z, 1 - yl, x), frm * 2 + k).wait_recv()

        core_copy(s, line).start()

        @pl.loop(0, 2)
        def _(kk):
            @pl.when(kk == 1)
            def _():
                at = L.at[tile_of(1 - k, line)]
                remote(at, at, ss.at[s], rs.at[s], c, sib).wait_recv()

            t = tile_of((k + kk) % 2, line)

            @pl.when(t <= 15 - t0)
            def _():
                LT[t] = L[t].astype(F32).T.astype(BF16)

            @pl.loop(0, 2)
            def _(i):
                @pl.when(((i == 0) & (t <= 15 - t0)) | ((i == 1) & (t <= t0)))
                def _():
                    forward(t, 1 - i)

    for hf in range(2):
        for ch in range(4):
            cs = slice(ch * 256, ch * 256 + 256)
            lse[hf, :, cs] = top[hf, :, cs] + jnp.log2(tot[hf, :, cs])
            o = O[hf, :, cs] * (1.0 / tot[hf, :, cs])
            O[hf, :, cs] = o
            delta[hf, :, cs] = jnp.sum(GT[hf, :, cs].astype(F32) * o, axis=0, keepdims=True)

    for d in (1, 2, 3):
        x_copy(d).wait_send()
        z_copy(d).wait_send()

    @pl.loop(0, 8)
    def _(s):
        dz, dy = order(s)

        @pl.when(dy == 0)
        def _():
            for to in range(2):
                y_copy(dz, to).wait_send()

        core_copy(s, line_at(dz, dy)).wait_send()

    def backward(t, hf):
        slot = slot_of(t, hf)
        for ch in range(4):
            cs = slice(ch * 256, ch * 256 + 256)
            dp = dot(L[t, :, :512], GT[hf, :, cs])
            p = jnp.exp2(S[slot, :, cs] - lse[hf, :, cs])
            dsb[:, cs] = (p * (dp - delta[hf, :, cs]) * SCALE).astype(BF16)
            pbb[:, cs] = p.astype(BF16)
        for ch in range(4):
            cs = slice(ch * 256, ch * 256 + 256)
            DA[hf, :, cs] += dot(LT[t], dsb[:, cs])
        a, b = dot(dsb[...], A[hf]), dot(pbb[...], G[hf])
        acc[:, :512] += a[:, :512] + b
        acc[:, 512:] += a[:, 512:]

    def r1_copy(s, line):
        return remote(L.at[tile_of(1 - k, line)], R1.at[s], s1.at[s], r1.at[s], c, sib)

    def r2_copy(s, line, dx):
        to = (x + dx) % 4
        return remote(L.at[tile_of(k, line), pl.ds(block_at(to), 64), :], R2.at[s, dx - 1],
                      s2.at[s, dx - 1], r2.at[s, dx - 1], cid(z, yl, to), tp)

    def r3_copy(s, to):
        dz, dy = order(s)
        slot = ((4 - dz) % 4) * 4 + dy * 2 + (yh + to) % 2
        return remote(R3s.at[s, 32 * to:32 * to + 32, :], R3.at[slot], s3.at[s, to], r3.at[slot],
                      cid((z + dz) % 4, (yl + dy) % 2, x), to * 2 + k)

    def finish(s):
        dz, dy = order(s)
        line = line_at(dz, dy)

        @pl.when(active(k, line))
        def _():
            for dx in (1, 2, 3):
                r2_copy(s, line, dx).wait_recv()
            total = L[tile_of(k, line), pl.ds(block_at(x), 64), :].astype(F32)
            for dx in range(3):
                total = total + R2[s, dx].astype(F32)
            R3s[s] = total.astype(BF16)
            for to in range(2):
                @pl.when((s > 0) | (yh != to))
                def _():
                    r3_copy(s, to).start()

                @pl.when((s == 0) & (yh == to))
                def _():
                    R3[0] = R3s[0, 32 * to:32 * to + 32, :]

    @pl.loop(0, 8)
    def _(i):
        s = 7 - i
        dz, dy = order(s)
        line = line_at(dz, dy)

        @pl.loop(0, 2)
        def _(kk):
            kind = (k + 1 - kk) % 2
            t = tile_of(kind, line)

            @pl.when((kk == 1) & (s < 7))
            def _():
                finish(s + 1)

            @pl.when(active(kind, line))
            def _():
                acc[...] = jnp.zeros_like(acc)

                @pl.loop(0, 2)
                def _(i):
                    @pl.when((i == 0) | (t <= t0))
                    def _():
                        backward(t, 1 - i)

                @pl.when(kk == 0)
                def _():
                    L[t] = acc[...].astype(BF16)
                    r1_copy(s, line).start()

                @pl.when(kk == 1)
                def _():
                    remote(L.at[t], R1.at[s], s1.at[s], r1.at[s], c, sib).wait_recv()
                    L[t] = (acc[...] + R1[s].astype(F32)).astype(BF16)
                    for dx in (1, 3, 2):
                        r2_copy(s, line, dx).start()

    @pl.loop(0, 8)
    def _(p):
        cols = pl.ds(pl.multiple_of(p * 128, 128), 128)
        ob = [O[hf, :, cols].T.astype(BF16) for hf in range(2)]
        db = [DA[hf, :, cols].T.astype(BF16) for hf in range(2)]
        for e in range(2):
            r = slice(64 * e, 64 * e + 64)
            h = 2 * p + e
            o = jnp.concatenate([ob[0][r], ob[1][r]], axis=0)
            d = jnp.concatenate([db[0][r], db[1][r]], axis=0)
            attn[h] = dot(o, wv[h]).astype(BF16)
            gq[h] = dot_nt(d[:, :512], wk[h]).astype(BF16)
            gqr[h] = d[:, 512:]

        @pl.when(p == 0)
        def _():
            finish(0)

    my_rows = pl.ds(pl.multiple_of(64 * k + 32 * yh, 32), 32)
    fin[my_rows, :] = R3[0].astype(F32)

    @pl.loop(1, 16)
    def _(slot):
        source = 2 * ((z + slot // 4) % 4) + (yl + (slot // 2) % 2) % 2

        @pl.when((k == 0) | (t0 >= source))
        def _():
            at = R3.at[slot]
            remote(at, at, s3.at[0, 0], r3.at[slot], c, sib).wait_recv()
            fin[my_rows, :] += at[...].astype(F32)

    def r4_copy(j):
        at = fin.at[my_rows, :]
        return remote(at, at, s4.at[j - 1], r4.at[j - 1], c, ((yh + j // 2) % 2) * 2 + (k + j % 2) % 2)

    for j in (1, 2, 3):
        r4_copy(j).start()

    @pl.loop(0, 8)
    def _(s):
        dz, dy = order(s)
        line = line_at(dz, dy)

        @pl.when(active(1 - k, line))
        def _():
            r1_copy(s, line).wait_send()

        @pl.when(active(k, line))
        def _():
            for dx in (1, 2, 3):
                r2_copy(s, line, dx).wait_send()
            for to in range(2):
                @pl.when((s > 0) | (yh != to))
                def _():
                    r3_copy(s, to).wait_send()

    for j in (1, 2, 3):
        r4_copy(j).wait()
    gl[...] = fin[...]


DMA = pltpu.SemaphoreType.DMA
SCRATCH = [
    pltpu.VMEM((16, 256, 576), BF16),
    pltpu.VMEM((16, 576, 256), BF16),
    pltpu.VMEM((2, 1024, 576), BF16),
    pltpu.VMEM((2, 576, 1024), BF16),
    pltpu.VMEM((2, 1024, 512), BF16),
    pltpu.VMEM((2, 512, 1024), BF16),
    pltpu.VMEM((17, 256, 1024), F32),
    pltpu.VMEM((2, 512, 1024), F32),
    pltpu.VMEM((2, 576, 1024), F32),
    pltpu.VMEM((2, 1, 1024), F32),
    pltpu.VMEM((2, 1, 1024), F32),
    pltpu.VMEM((2, 1, 1024), F32),
    pltpu.VMEM((2, 1, 1024), F32),
    pltpu.VMEM((256, 1024), BF16),
    pltpu.VMEM((256, 1024), BF16),
    pltpu.VMEM((256, 576), F32),
    pltpu.VMEM((8, 256, 576), BF16),
    pltpu.VMEM((8, 3, 64, 576), BF16),
    pltpu.VMEM((8, 64, 576), BF16),
    pltpu.VMEM((16, 32, 576), BF16),
    pltpu.VMEM((128, 576), F32),
    DMA((3,)), DMA((3,)), DMA((3,)), DMA((3,)), DMA((4, 2)), DMA((4, 2)), DMA((8,)), DMA((8,)),
    DMA((8,)), DMA((8,)), DMA((8, 3)), DMA((8, 3)), DMA((8, 2)), DMA((16,)), DMA((3,)), DMA((3,)),
]


def body(q_nope, q_rope, latent, up_keys, up_values, out_grad):
    def heads(v):
        return jnp.swapaxes(v, 0, 1)

    vmem = pl.BlockSpec(memory_space=pltpu.VMEM)
    attn, gq, gqr, gl = pl.pallas_call(
        kernel,
        out_shape=[
            jax.ShapeDtypeStruct((16, 128, 128), BF16),
            jax.ShapeDtypeStruct((16, 128, 128), BF16),
            jax.ShapeDtypeStruct((16, 128, 64), BF16),
            jax.ShapeDtypeStruct((128, 576), F32),
        ],
        in_specs=[vmem] * 6,
        out_specs=[vmem] * 4,
        scratch_shapes=SCRATCH,
        compiler_params=pltpu.CompilerParams(
            vmem_limit_bytes=63 * 2**20, collective_id=0, has_side_effects=True),
        cost_estimate=pl.CostEstimate(flops=30_000_000_000, bytes_accessed=12_000_000, transcendentals=9_000_000),
    )(latent, heads(q_nope), heads(q_rope), heads(out_grad), up_keys, up_values)
    return heads(attn), heads(gq), heads(gqr), gl


def solution(mesh):
    rows = P("ctx", "tp", None)
    return jax.shard_map(
        body, mesh=mesh,
        in_specs=(rows, rows, P("ctx", None), P("tp", None, None), P("tp", None, None), rows),
        out_specs=(rows, rows, rows, P("ctx", None)),
        check_vma=False,
    )
```

time: 470 us -> 135 us (0.29)
  waiting for transfers between devices: 368 us -> 0 us
  Pallas kernels: 64 us -> 120 us
  between operations: 13.8 us -> 0.66 us
  other arithmetic: 6.58 us -> 0 us
  local copies, waits for them, and re-layouts: 17.5 us -> 12.3 us
    reduce_scatter x1 -> x0, waiting for transfers between devices: 168 us -> none  [body(): part = lax.psum_scatter(dl, 'ctx', scatter_dimension=0, tiled=True)]
    all_gather x1 -> x0, waiting for transfers between devices: 141 us -> none  [body(): lax.all_gather(latent, 'ctx', axis=0, tiled=True).reshape(32, 2, 64, 576)]
    psum x1 -> x0, waiting for transfers between devices: 59 us -> none  [body(): lax.psum(part, 'tp').astype(F32)]
    pallas_call x1, Pallas kernels: 64 us -> 120 us  [body(): pl.pallas_call(kernel, out_shape=[jax.ShapeDtypeStruct((16, 128, 128), BF...]
    unnamed x12 -> x10, local copies, waits for them, and re-layouts: 8.62 us -> 9.86 us
  transfers between devices with their start and end apart: 3 -> 0, of which waited for: 3 -> 0; matrix products, arithmetic and copies ran while one was open for 2% -> 0% of each run, Pallas kernels for 0% -> 0%
where the time goes in v2:
time: 135 us; the launch traced here: 133 us
  Pallas kernels  120 us (89%)
  local copies, waits for them, and re-layouts  12.3 us (9%)
    pallas_call x1, Pallas kernels, body(): pl.pallas_call(kernel, out_shape=[jax.ShapeDtypeStruct((16, 128, 128), BF...  120 us
    unnamed x10, local copies, waits for them, and re-layouts  9.86 us

profile of v2, /device:TPU:1, one launch (start us, length us, event | category | flops | bytes accessed | tf_op | source)
XLA Modules:
  0.0 132.8 jit_solution(2205672669605056854)
XLA Ops:
  0.6 1.7 %copy.13.lat = bf16[128,576]{1,0:T(8,128)(2,1)} copy(bf16[128,576]{0,1:T(8,128)(2,1)} %param.8) | data formatting | bytes 294912 | tf_op args[2]
  2.3 1.9 %copy.11 = bf16[128,16,64]{2,0,1:T(8,128)(2,1)} copy(bf16[128,16,64]{0,2,1:T(8,128)(2,1)} %param.7) | data formatting | bytes 524288 | tf_op args[1]
  4.3 2.4 %copy_bitcast_fusion = (bf16[16,128,128]{2,1,0:T(8,128)(2,1)}, bf16[16,128,128]{2,1,0:T(8,128)(2,1)}) fusion(bf16[128,16,128]{2,1,0:T(8,128)(2,1)} %param.11, bf16[128,16,128]{2,1,0:T(8,128)(2,1)} %param.6), kind=kLoop, calls=%fused_computation | loop fusion | bytes 2097152 | tf_op jit(solution)/shard_map/transpose | solution.py:400
  6.7 119.9 %shard_map.93 = (bf16[16,128,128]{2,1,0:T(8,128)(2,1)}, bf16[16,128,128]{2,1,0:T(8,128)(2,1)}, bf16[16,128,64]{2,1,0:T(8,128)(2,1)}, f32[128,576]{1,0:T(8,128)}) custom-call(bf16[128,576]{1,0:T(8,128)(2,1)} %copy.13.lat, bf16[16,128,128]{2,1,0:T(8,128)(2,1)} %get-tuple-element.17.q, bf16[16,128,64]{2,1,0:T(8,128)(2,1)} %bitcast.9, ...), custom_call_target="tpu_custom_call" | custom-call | flops 30000001024 | bytes 12000000 | tf_op jit(solution)/shard_map/pallas_call | solution.py:403
  126.6 0.0 copy-start
  126.6 0.0 copy-start.1
  126.6 2.3 %copy.14 = bf16[128,16,128]{2,1,0:T(8,128)(2,1)} copy(bf16[128,16,128]{2,0,1:T(8,128)(2,1)} %bitcast.11) | data formatting | bytes 1048576
  128.9 2.2 %copy.15 = bf16[128,16,128]{2,1,0:T(8,128)(2,1)} copy(bf16[128,16,128]{2,0,1:T(8,128)(2,1)} %bitcast.10) | data formatting | bytes 1048576
  131.1 0.0 copy-done
  131.1 0.9 copy.16
  132.0 0.0 copy-done.1
  132.0 0.9 copy.17
Async XLA Ops:
  126.6 4.4 %copy-start = (bf16[16,128,64]{2,1,0:T(8,128)(2,1)S(1)}, bf16[16,128,64]{2,1,0:T(8,128)(2,1)}, u32[]{:S(2)}) copy-start(bf16[16,128,64]{2,1,0:T(8,128)(2,1)} %get-tuple-element.10) | copy-start | bytes 786436
  126.6 5.3 %copy-start.1 = (f32[128,576]{1,0:T(8,128)S(1)}, f32[128,576]{1,0:T(8,128)}, u32[]{:S(2)}) copy-start(f32[128,576]{1,0:T(8,128)} %get-tuple-element.15) | copy-start | bytes 884740

commit v3 on v2

--- a/solution.py
+++ b/solution.py
@@ -29,10 +29,11 @@
     )
 
 
-def kernel(lat, q, qr, og, wk, wv, attn, gq, gqr, gl,
+def kernel(lat_hbm, q_hbm, qr_hbm, og_hbm, wk_hbm, wv_hbm, attn_hbm, gq_hbm, gqr_hbm, gl_hbm,
+           lat, q, qr, og, wk, wv, X, sin, sout,
            L, LT, A, AT, G, GT, S, O, DA, top, tot, lse, delta, dsb, pbb, acc,
-           R1, R2, R3s, R3, fin,
-           sx, rx, sz, rz, sy, ry, ss, rs, s1, r1, s2, r2, s3, r3, s4, r4):
+           R1, R2, R3s, R3, fin, flip,
+           sx, rx, sz, rz, sb, rb, sy, ry, ss, rs, s1, r1, s2, r2, s3, r3, s4, r4):
     c, tp = lax.axis_index("ctx"), lax.axis_index("tp")
     z, yl, x = c // 8, (c // 4) % 2, c % 4
     yh, k = tp // 2, tp % 2
@@ -49,14 +50,24 @@
         return pl.multiple_of(64 * jnp.where(k == 0, x_, 3 - x_), 64)
 
     def order(s):
-        i = s % 4
-        return i + jnp.where(i == 2, 1, 0) - jnp.where(i == 3, 1, 0), s // 4
+        i = jnp.where(s >= 5, s - 4, s - 1)
+        dz = i + jnp.where(i == 2, 1, 0) - jnp.where(i == 3, 1, 0)
+        return jnp.where(s <= 1, 0, dz), jnp.where((s == 1) | (s >= 5), 1, 0)
 
     def line_at(dz, dy):
         return 2 * ((z + dz) % 4) + (yl + dy) % 2
 
     def active(kind, line):
         return (kind == 0) | (line >= t0)
+
+    mine = tile_of(k, t0)
+    loads = [
+        pltpu.make_async_copy(src, dst, sin.at[i]) for i, (src, dst) in enumerate((
+            (lat_hbm, lat),
+            (q_hbm, q), (wk_hbm, wk), (qr_hbm, qr), (og_hbm, og), (wv_hbm, wv)))
+    ]
+    for load in loads:
+        load.start()
 
     barrier = pltpu.get_barrier_semaphore()
 
@@ -75,8 +86,6 @@
     hello(c, (1 - yh) * 2 + 1 - k)
     pl.semaphore_wait(barrier, 20)
 
-    mine = tile_of(k, t0)
-
     def x_copy(dx):
         at = L.at[mine, pl.ds(block_at(x), 64), :]
         return remote(at, at, sx.at[dx - 1], rx.at[dx - 1], cid(z, yl, (x + dx) % 4), tp)
@@ -85,6 +94,24 @@
         at = L.at[mine]
         return remote(at, at, sz.at[dz - 1], rz.at[3 - dz], cid((z + dz) % 4, yl, x), tp)
 
+    def zb_copy(dz):
+        at = L.at[mine, pl.ds(block_at(x), 64), :]
+        return remote(at, at, sz.at[dz - 1], rz.at[3 - dz], cid((z + dz) % 4, yl, x), tp)
+
+    def xb_copy(dz, dx):
+        at = L.at[tile_of(k, line_at(dz, 0)), pl.ds(block_at(x), 64), :]
+        return remote(at, at, sb.at[dz - 1, dx - 1], rb.at[dz - 1, dx - 1], cid(z, yl, (x + dx) % 4), tp)
+
+    def wait_line(dz):
+        @pl.when(k == 0)
+        def _():
+            z_copy(4 - dz).wait_recv()
+
+        @pl.when(k == 1)
+        def _():
+            for dx in (1, 3, 2):
+                xb_copy(dz, dx).wait_recv()
+
     def y_copy(dz, to):
         at = L.at[tile_of(k, line_at(dz, 0)), pl.ds(pl.multiple_of(128 * yh, 128), 128), :]
         return remote(at, at, sy.at[dz, to], ry.at[dz, yh], cid(z, 1 - yl, x), to * 2 + k)
@@ -93,26 +120,41 @@
         at = L.at[tile_of(k, line)]
         return remote(at, at, ss.at[s], rs.at[s], c, sib)
 
-    L[mine, pl.ds(block_at(x), 64), :] = lat[pl.ds(pl.multiple_of(64 * k, 64), 64), :]
+    loads[0].wait()
+    fin[...] = lat[...].astype(F32).T
+    L[mine, pl.ds(block_at(x), 64), :] = fin[pl.ds(pl.multiple_of(64 * k, 64), 64), :].astype(BF16)
     for dx in (1, 3, 2):
         x_copy(dx).start()
+
+    @pl.when(k == 1)
+    def _():
+        for dz in (1, 3, 2):
+            zb_copy(dz).start()
+
+    for load in loads[1:]:
+        load.wait()
+    X[0] = q[...].astype(F32)
+    X[1] = og[...].astype(F32)
+
+    def head(i, h):
+        return X[i, pl.ds(h, 128, stride=16), :]
 
     @pl.loop(0, 8)
     def _(p):
         cols = pl.ds(pl.multiple_of(p * 128, 128), 128)
-        pa = dot(q[2 * p], wk[2 * p])
-        pb = dot(q[2 * p + 1], wk[2 * p + 1])
-        ga = dot_nt(og[2 * p], wv[2 * p])
-        gb = dot_nt(og[2 * p + 1], wv[2 * p + 1])
-        ra, rb = qr[2 * p], qr[2 * p + 1]
+        pa = dot(head(0, 2 * p).astype(BF16), wk[2 * p])
+        pb = dot(head(0, 2 * p + 1).astype(BF16), wk[2 * p + 1])
+        ga = dot_nt(head(1, 2 * p).astype(BF16), wv[2 * p])
+        gb = dot_nt(head(1, 2 * p + 1).astype(BF16), wv[2 * p + 1])
+        ra, rb = qr[2 * p].astype(F32).T, qr[2 * p + 1].astype(F32).T
         for hf in range(2):
             r = slice(64 * hf, 64 * hf + 64)
             blk = jnp.concatenate([pa[r], pb[r]], axis=0)
             A[hf, cols, :512] = blk.astype(BF16)
             AT[hf, :512, cols] = blk.T.astype(BF16)
             rblk = jnp.concatenate([ra[r], rb[r]], axis=0)
-            A[hf, cols, 512:] = rblk
-            AT[hf, 512:, cols] = rblk.astype(F32).T.astype(BF16)
+            A[hf, cols, 512:] = rblk.astype(BF16)
+            AT[hf, 512:, cols] = rblk.T.astype(BF16)
             gblk = jnp.concatenate([ga[r], gb[r]], axis=0)
             G[hf, cols, :] = gblk.astype(BF16)
             GT[hf, :, cols] = gblk.T.astype(BF16)
@@ -152,30 +194,51 @@
 
     for dx in (1, 2, 3):
         x_copy(dx).wait_recv()
-    for dz in (1, 3, 2):
-        z_copy(dz).start()
+    @pl.when(k == 0)
+    def _():
+        for dz in (1, 3):
+            z_copy(dz).start()
+
+    def pass_on(s, dz):
+        for to in range(2):
+            y_copy(dz, to).start()
+        core_copy(s, line_at(dz, 0)).start()
+
+    pass_on(0, 0)
+
+    @pl.when(k == 1)
+    def _():
+        for dz in (1, 3, 2):
+            zb_copy(4 - dz).wait_recv()
+            for dx in (1, 3, 2):
+                xb_copy(dz, dx).start()
 
     @pl.loop(0, 8)
     def _(s):
         dz, dy = order(s)
         line = line_at(dz, dy)
 
-        @pl.when((dy == 0) & (dz > 0))
-        def _():
-            z_copy(4 - dz).wait_recv()
-
-        @pl.when(dy == 0)
-        def _():
-            for to in range(2):
-                y_copy(dz, to).start()
+        @pl.when((s == 1) & (k == 0))
+        def _():
+            z_copy(2).start()
+
+        @pl.when(s == 2)
+        def _():
+            for at, dz_ in ((2, 1), (3, 3)):
+                wait_line(dz_)
+                pass_on(at, dz_)
+
+        @pl.when(s == 4)
+        def _():
+            wait_line(2)
+            pass_on(4, 2)
 
         @pl.when(dy == 1)
         def _():
             for frm in range(2):
                 at = L.at[tile_of(k, line), 128 * frm:128 * frm + 128, :]
                 remote(at, at, sy.at[dz, 0], ry.at[dz, frm], cid(z, 1 - yl, x), frm * 2 + k).wait_recv()
-
-        core_copy(s, line).start()
+            core_copy(s, line).start()
 
         @pl.loop(0, 2)
         def _(kk):
@@ -206,7 +269,16 @@
 
     for d in (1, 2, 3):
         x_copy(d).wait_send()
-        z_copy(d).wait_send()
+
+        @pl.when(k == 0)
+        def _():
+            z_copy(d).wait_send()
+
+        @pl.when(k == 1)
+        def _():
+            zb_copy(d).wait_send()
+            for dx in (1, 2, 3):
+                xb_copy(d, dx).wait_send()
 
     @pl.loop(0, 8)
     def _(s):
@@ -237,37 +309,103 @@
     def r1_copy(s, line):
         return remote(L.at[tile_of(1 - k, line)], R1.at[s], s1.at[s], r1.at[s], c, sib)
 
-    def r2_copy(s, line, dx):
+    def r2x_copy(s, line, dx):
         to = (x + dx) % 4
-        return remote(L.at[tile_of(k, line), pl.ds(block_at(to), 64), :], R2.at[s, dx - 1],
-                      s2.at[s, dx - 1], r2.at[s, dx - 1], cid(z, yl, to), tp)
-
-    def r3_copy(s, to):
+        return remote(L.at[tile_of(k, line), pl.ds(block_at(to), 64), :], R2.at[s * 3 + dx - 1],
+                      s2.at[s, dx], r2.at[s * 3 + dx - 1], cid(z, yl, to), tp)
+
+    def r2z_copy(s, line, dz, dy, b):
+        slot = ((3 - dz) * 2 + dy) * 4 + b
+        return remote(L.at[tile_of(k, line), 64 * b:64 * b + 64, :], R2.at[slot],
+                      s2.at[s, b], r2.at[slot], cid((z + dz) % 4, yl, x), tp)
+
+    def r2_each(s, line, do):
+        dz, dy = order(s)
+
+        @pl.when((k == 0))
+        def _():
+            for dx in (1, 3, 2):
+                do(r2x_copy(s, line, dx))
+
+        @pl.when((k == 1) & (dz > 0))
+        def _():
+            for b in range(4):
+                do(r2z_copy(s, line, dz, dy, b))
+
+    def r3x_copy(s, to):
         dz, dy = order(s)
         slot = ((4 - dz) % 4) * 4 + dy * 2 + (yh + to) % 2
         return remote(R3s.at[s, 32 * to:32 * to + 32, :], R3.at[slot], s3.at[s, to], r3.at[slot],
                       cid((z + dz) % 4, (yl + dy) % 2, x), to * 2 + k)
 
-    def finish(s):
+    def r3x_each(s, do):
+        for to in range(2):
+            @pl.when((s > 0) | (yh != to))
+            def _():
+                do(r3x_copy(s, to))
+
+    def finish_x(s):
         dz, dy = order(s)
         line = line_at(dz, dy)
-
-        @pl.when(active(k, line))
-        def _():
-            for dx in (1, 2, 3):
-                r2_copy(s, line, dx).wait_recv()
-            total = L[tile_of(k, line), pl.ds(block_at(x), 64), :].astype(F32)
-            for dx in range(3):
-                total = total + R2[s, dx].astype(F32)
-            R3s[s] = total.astype(BF16)
+        for dx in (1, 2, 3):
+            r2x_copy(s, line, dx).wait_recv()
+        total = L[tile_of(k, line), pl.ds(block_at(x), 64), :].astype(F32)
+        for dx in range(3):
+            total = total + R2[s * 3 + dx].astype(F32)
+        R3s[s] = total.astype(BF16)
+        r3x_each(s, lambda copy: copy.start())
+
+        @pl.when(s == 0)
+        def _():
+            R3[0] = R3s[0, pl.ds(pl.multiple_of(32 * yh, 32), 32), :]
+
+    def r3z_copy(dx, dy, to):
+        at = L.at[tile_of(k, line_at(0, dy)), pl.ds(pl.multiple_of(block_at((x + dx) % 4) + 32 * to, 32), 32), :]
+        slot = ((4 - dx) % 4) * 4 + dy * 2 + (yh + to) % 2
+        return remote(at, R3.at[slot], s3.at[dx * 2 + dy, to], r3.at[slot],
+                      cid(z, (yl + dy) % 2, (x + dx) % 4), to * 2 + k)
+
+    def z_any(dy):
+        return (yl + dy) % 2 + z >= yl
+
+    def r3z_each(dy, do):
+        for dx in (2, 1, 3, 0):
             for to in range(2):
-                @pl.when((s > 0) | (yh != to))
+                if dx == 0 and dy == 0:
+                    @pl.when(yh != to)
+                    def _():
+                        do(r3z_copy(dx, dy, to))
+                else:
+                    do(r3z_copy(dx, dy, to))
+
+    def finish_z(dy):
+        line = line_at(0, dy)
+
+        @pl.when(z_any(dy))
+        def _():
+            t = tile_of(k, line)
+
+            @pl.when(line >= t0)
+            def _():
+                acc[...] = L[t].astype(F32)
+
+            @pl.when(line < t0)
+            def _():
+                acc[...] = jnp.zeros_like(acc)
+
+            for off in (1, 2, 3):
+                @pl.when((z + off) % 4 < z)
                 def _():
-                    r3_copy(s, to).start()
-
-                @pl.when((s == 0) & (yh == to))
-                def _():
-                    R3[0] = R3s[0, 32 * to:32 * to + 32, :]
+                    for b in range(4):
+                        slot = ((off - 1) * 2 + dy) * 4 + b
+                        at = R2.at[slot]
+                        remote(at, at, s2.at[0, 0], r2.at[slot], c, sib).wait_recv()
+                        acc[64 * b:64 * b + 64, :] += at[...].astype(F32)
+
+            L[t] = acc[...].astype(BF16)
+            r3z_each(dy, lambda copy: copy.start())
+            if dy == 0:
+                R3[0] = L[t, pl.ds(pl.multiple_of(block_at(x) + 32 * yh, 32), 32), :]
 
     @pl.loop(0, 8)
     def _(i):
@@ -280,9 +418,9 @@
             kind = (k + 1 - kk) % 2
             t = tile_of(kind, line)
 
-            @pl.when((kk == 1) & (s < 7))
-            def _():
-                finish(s + 1)
+            @pl.when((kk == 1) & (s < 6) & (k == 0))
+            def _():
+                finish_x(s + 2)
 
             @pl.when(active(kind, line))
             def _():
@@ -303,8 +441,12 @@
                 def _():
                     remote(L.at[t], R1.at[s], s1.at[s], r1.at[s], c, sib).wait_recv()
                     L[t] = (acc[...] + R1[s].astype(F32)).astype(BF16)
-                    for dx in (1, 3, 2):
-                        r2_copy(s, line, dx).start()
+                    r2_each(s, line, lambda copy: copy.start())
+
+    @pl.when(k == 1)
+    def _():
+        finish_z(1)
+        finish_z(0)
 
     @pl.loop(0, 8)
     def _(p):
@@ -316,22 +458,29 @@
             h = 2 * p + e
             o = jnp.concatenate([ob[0][r], ob[1][r]], axis=0)
             d = jnp.concatenate([db[0][r], db[1][r]], axis=0)
-            attn[h] = dot(o, wv[h]).astype(BF16)
-            gq[h] = dot_nt(d[:, :512], wk[h]).astype(BF16)
-            gqr[h] = d[:, 512:]
-
-        @pl.when(p == 0)
-        def _():
-            finish(0)
+            rows = pl.ds(h, 128, stride=16)
+            X[0, rows, :] = dot(o, wv[h])
+            X[1, rows, :] = dot_nt(d[:, :512], wk[h])
+            qr[h] = d[:, 512:].astype(F32).T.astype(BF16)
+
+        @pl.when((p == 0) & (k == 0))
+        def _():
+            finish_x(1)
+            finish_x(0)
+
+    stores = []
+    q[...] = X[0].astype(BF16)
+    og[...] = X[1].astype(BF16)
+    for i, (ref, out) in enumerate(((q, attn_hbm), (og, gq_hbm), (qr, gqr_hbm))):
+        stores.append(pltpu.make_async_copy(ref, out, sout.at[i]))
+        stores[i].start()
 
     my_rows = pl.ds(pl.multiple_of(64 * k + 32 * yh, 32), 32)
     fin[my_rows, :] = R3[0].astype(F32)
 
     @pl.loop(1, 16)
     def _(slot):
-        source = 2 * ((z + slot // 4) % 4) + (yl + (slot // 2) % 2) % 2
-
-        @pl.when((k == 0) | (t0 >= source))
+        @pl.when((k == 0) | (z + yl >= (yl + (slot // 2) % 2) % 2))
         def _():
             at = R3.at[slot]
             remote(at, at, s3.at[0, 0], r3.at[slot], c, sib).wait_recv()
@@ -355,20 +504,38 @@
 
         @pl.when(active(k, line))
         def _():
-            for dx in (1, 2, 3):
-                r2_copy(s, line, dx).wait_send()
-            for to in range(2):
-                @pl.when((s > 0) | (yh != to))
-                def _():
-                    r3_copy(s, to).wait_send()
+            r2_each(s, line, lambda copy: copy.wait_send())
+
+        @pl.when(k == 0)
+        def _():
+            r3x_each(s, lambda copy: copy.wait_send())
+
+    @pl.when(k == 1)
+    def _():
+        for dy in range(2):
+            @pl.when(z_any(dy))
+            def _():
+                r3z_each(dy, lambda copy: copy.wait_send())
 
     for j in (1, 2, 3):
         r4_copy(j).wait()
-    gl[...] = fin[...]
+    flip[...] = fin[...].T
+    stores.append(pltpu.make_async_copy(flip, gl_hbm, sout.at[3]))
+    stores[3].start()
+    for store in stores:
+        store.wait()
 
 
 DMA = pltpu.SemaphoreType.DMA
 SCRATCH = [
+    pltpu.VMEM((576, 128), BF16),
+    pltpu.VMEM((2048, 128), BF16),
+    pltpu.VMEM((16, 64, 128), BF16),
+    pltpu.VMEM((2048, 128), BF16),
+    pltpu.VMEM((16, 128, 512), BF16),
+    pltpu.VMEM((16, 512, 128), BF16),
+    pltpu.VMEM((2, 2048, 128), F32),
+    DMA((6,)), DMA((4,)),
     pltpu.VMEM((16, 256, 576), BF16),
     pltpu.VMEM((16, 576, 256), BF16),
     pltpu.VMEM((2, 1024, 576), BF16),
@@ -386,36 +553,37 @@
     pltpu.VMEM((256, 1024), BF16),
     pltpu.VMEM((256, 576), F32),
     pltpu.VMEM((8, 256, 576), BF16),
-    pltpu.VMEM((8, 3, 64, 576), BF16),
+    pltpu.VMEM((24, 64, 576), BF16),
     pltpu.VMEM((8, 64, 576), BF16),
     pltpu.VMEM((16, 32, 576), BF16),
     pltpu.VMEM((128, 576), F32),
-    DMA((3,)), DMA((3,)), DMA((3,)), DMA((3,)), DMA((4, 2)), DMA((4, 2)), DMA((8,)), DMA((8,)),
-    DMA((8,)), DMA((8,)), DMA((8, 3)), DMA((8, 3)), DMA((8, 2)), DMA((16,)), DMA((3,)), DMA((3,)),
+    pltpu.VMEM((576, 128), F32),
+    DMA((3,)), DMA((3,)), DMA((3,)), DMA((3,)), DMA((3, 3)), DMA((3, 3)), DMA((4, 2)), DMA((4, 2)), DMA((8,)), DMA((8,)),
+    DMA((8,)), DMA((8,)), DMA((8, 4)), DMA((24,)), DMA((8, 2)), DMA((16,)), DMA((3,)), DMA((3,)),
 ]
 
 
 def body(q_nope, q_rope, latent, up_keys, up_values, out_grad):
-    def heads(v):
-        return jnp.swapaxes(v, 0, 1)
-
-    vmem = pl.BlockSpec(memory_space=pltpu.VMEM)
+    def flat(v):
+        return v.reshape(2048, v.shape[2])
+
+    hbm = pl.BlockSpec(memory_space=pl.ANY)
     attn, gq, gqr, gl = pl.pallas_call(
         kernel,
         out_shape=[
-            jax.ShapeDtypeStruct((16, 128, 128), BF16),
-            jax.ShapeDtypeStruct((16, 128, 128), BF16),
-            jax.ShapeDtypeStruct((16, 128, 64), BF16),
-            jax.ShapeDtypeStruct((128, 576), F32),
+            jax.ShapeDtypeStruct((2048, 128), BF16),
+            jax.ShapeDtypeStruct((2048, 128), BF16),
+            jax.ShapeDtypeStruct((16, 64, 128), BF16),
+            jax.ShapeDtypeStruct((576, 128), F32),
         ],
-        in_specs=[vmem] * 6,
-        out_specs=[vmem] * 4,
+        in_specs=[hbm] * 6,
+        out_specs=[hbm] * 4,
         scratch_shapes=SCRATCH,
         compiler_params=pltpu.CompilerParams(
             vmem_limit_bytes=63 * 2**20, collective_id=0, has_side_effects=True),
         cost_estimate=pl.CostEstimate(flops=30_000_000_000, bytes_accessed=12_000_000, transcendentals=9_000_000),
-    )(latent, heads(q_nope), heads(q_rope), heads(out_grad), up_keys, up_values)
-    return heads(attn), heads(gq), heads(gqr), gl
+    )(latent.T, flat(q_nope), jnp.transpose(q_rope, (1, 2, 0)), flat(out_grad), up_keys, up_values)
+    return attn.reshape(128, 16, 128), gq.reshape(128, 16, 128), jnp.transpose(gqr, (2, 0, 1)), gl.T
 
 
 def solution(mesh):

time: 135 us -> 95.1 us (0.70)
  the two profiles are of different devices: /device:TPU:1 before, /device:TPU:73 now
where the time goes in v3:
time: 95.1 us; the launch traced here: 95 us
  Pallas kernels  89.1 us (94%)
  local copies, waits for them, and re-layouts  5.22 us (5%)
    pallas_call x1, Pallas kernels, body(): pl.pallas_call(kernel, out_shape=[jax.ShapeDtypeStruct((2048, 128), BF16)...  89.1 us
    unnamed x8, local copies, waits for them, and re-layouts  5.22 us

profile of v3, /device:TPU:73, one launch (start us, length us, event | category | flops | bytes accessed | tf_op | source)
XLA Modules:
  0.0 95.0 jit_solution(7569316764669974903)
XLA Ops:
  0.6 89.1 %shard_map.93 = (bf16[2048,128]{1,0:T(8,128)(2,1)}, bf16[2048,128]{1,0:T(8,128)(2,1)}, bf16[16,64,128]{2,1,0:T(8,128)(2,1)}, f32[576,128]{1,0:T(8,128)}) custom-call(bf16[576,128]{1,0:T(8,128)(2,1)} %bitcast.15, bf16[2048,128]{1,0:T(8,128)(2,1)} %bitcast.12, bf16[16,64,128]{2,1,0:T(8,128)(2,1)} %bitcast.14, bf16[2048,128]{1,0:T(8,128)(2,1)} %bitcast.13, ...), custom_call_target="tpu_custom_call" | custom-call | flops 30000001024 | bytes 12000000 | tf_op jit(solution)/shard_map/pallas_call | solution.py:571
  89.7 0.0 copy-start.1
  89.7 0.0 copy-start
  89.7 1.9 %copy.14 = bf16[128,16,128]{2,1,0:T(8,128)(2,1)} copy(bf16[128,16,128]{2,1,0:T(8,128)(2,1)} %bitcast.9) | data formatting | bytes 1048576
  91.7 1.9 %copy.15 = bf16[128,16,128]{2,1,0:T(8,128)(2,1)} copy(bf16[128,16,128]{2,1,0:T(8,128)(2,1)} %bitcast.8) | data formatting | bytes 1048576
  93.5 0.0 copy-done.1
  93.5 0.7 copy.16
  94.2 0.0 copy-done
  94.2 0.7 copy.17
Async XLA Ops:
  89.7 3.8 %copy-start.1 = (bf16[16,64,128]{2,1,0:T(8,128)(2,1)S(1)}, bf16[16,64,128]{2,1,0:T(8,128)(2,1)}, u32[]{:S(2)}) copy-start(bf16[16,64,128]{2,1,0:T(8,128)(2,1)} %get-tuple-element.10) | copy-start | bytes 786436
  89.7 4.5 %copy-start = (f32[576,128]{1,0:T(8,128)S(1)}, f32[576,128]{1,0:T(8,128)}, u32[]{:S(2)}) copy-start(f32[576,128]{1,0:T(8,128)} %get-tuple-element.11) | copy-start | bytes 884740

commit v4 on v3

--- a/solution.py
+++ b/solution.py
@@ -30,8 +30,8 @@
 
 
 def kernel(lat_hbm, q_hbm, qr_hbm, og_hbm, wk_hbm, wv_hbm, attn_hbm, gq_hbm, gqr_hbm, gl_hbm,
-           lat, q, qr, og, wk, wv, X, sin, sout,
-           L, LT, A, AT, G, GT, S, O, DA, top, tot, lse, delta, dsb, pbb, acc,
+           lat, q, qr, og, wk, wv, sin, sout,
+           L, LT, A, AT, G, GT, SA, SB, O, DA, top, tot, lse, delta, dsb, pbb, acc,
            R1, R2, R3s, R3, fin, flip,
            sx, rx, sz, rz, sb, rb, sy, ry, ss, rs, s1, r1, s2, r2, s3, r3, s4, r4):
     c, tp = lax.axis_index("ctx"), lax.axis_index("tp")
@@ -90,27 +90,24 @@
         at = L.at[mine, pl.ds(block_at(x), 64), :]
         return remote(at, at, sx.at[dx - 1], rx.at[dx - 1], cid(z, yl, (x + dx) % 4), tp)
 
-    def z_copy(dz):
-        at = L.at[mine]
-        return remote(at, at, sz.at[dz - 1], rz.at[3 - dz], cid((z + dz) % 4, yl, x), tp)
+    def z_copy(dz, part):
+        at = L.at[mine, pl.ds(pl.multiple_of(128 * ((yh + part) % 2), 128), 128), :]
+        return remote(at, at, sz.at[dz - 1, part], rz.at[3 - dz, part], cid((z + dz) % 4, yl, x), tp)
 
     def zb_copy(dz):
         at = L.at[mine, pl.ds(block_at(x), 64), :]
-        return remote(at, at, sz.at[dz - 1], rz.at[3 - dz], cid((z + dz) % 4, yl, x), tp)
+        return remote(at, at, sz.at[dz - 1, 0], rz.at[3 - dz, 0], cid((z + dz) % 4, yl, x), tp)
 
     def xb_copy(dz, dx):
         at = L.at[tile_of(k, line_at(dz, 0)), pl.ds(block_at(x), 64), :]
         return remote(at, at, sb.at[dz - 1, dx - 1], rb.at[dz - 1, dx - 1], cid(z, yl, (x + dx) % 4), tp)
 
-    def wait_line(dz):
-        @pl.when(k == 0)
-        def _():
-            z_copy(4 - dz).wait_recv()
-
-        @pl.when(k == 1)
-        def _():
-            for dx in (1, 3, 2):
-                xb_copy(dz, dx).wait_recv()
+    def xb_arrive(dz):
+        for dx in (1, 3, 2):
+            xb_copy(dz, dx).wait_recv()
+
+    def z_arrive(dz, part):
+        z_copy(4 - dz, part).wait_recv()
 
     def y_copy(dz, to):
         at = L.at[tile_of(k, line_at(dz, 0)), pl.ds(pl.multiple_of(128 * yh, 128), 128), :]
@@ -133,11 +130,11 @@
 
     for load in loads[1:]:
         load.wait()
-    X[0] = q[...].astype(F32)
-    X[1] = og[...].astype(F32)
+    SA[0:2048] = q[...].astype(F32)
+    SA[2048:4096] = og[...].astype(F32)
 
     def head(i, h):
-        return X[i, pl.ds(h, 128, stride=16), :]
+        return SA[pl.ds(2048 * i + h, 128, stride=16), :]
 
     @pl.loop(0, 8)
     def _(p):
@@ -164,47 +161,67 @@
     O[...] = jnp.zeros_like(O)
     DA[...] = jnp.zeros_like(DA)
 
-    def slot_of(t, hf):
-        return jnp.where(hf == 1, t, 16 - t)
-
-    def forward(t, hf):
-        slot = slot_of(t, hf)
-        base = jnp.where(hf == 1, 63 - c, c) * 64 - t * 256
-        diff = lax.broadcasted_iota(jnp.int32, (256, 256), 0) - lax.rem(
-            lax.broadcasted_iota(jnp.int32, (256, 256), 1), 64)
+    def units_of(line):
+        early = line <= t0
+        return ((0, line, 1, SA, line * 2048),
+                (1, jnp.where(early, line, 15 - line), jnp.where(early, 0, 1), SB, line * 2048))
+
+    third = (1, 15 - t0, 1, SB, 8 * 2048)
+
+    def score_at(row, ch, j):
+        return pl.ds(pl.multiple_of(row + ch * 512 + j * 256, 256), 256)
+
+    def score_load(ref, row, ch):
+        return jnp.concatenate([ref[score_at(row, ch, 0), :], ref[score_at(row, ch, 1), :]], axis=1)
+
+    def scores(unit, masked):
+        u, t, hf, ref, row = unit
         for ch in range(4):
             cs = slice(ch * 256, ch * 256 + 256)
-            s = dot(L[t], AT[hf, :, cs]) * LOG2_SCALE
-            S[slot, :, cs] = jnp.where(diff <= base, s, NEG)
+            v = dot(L[t], AT[hf, :, cs]) * LOG2_SCALE
+            if masked:
+                base = jnp.where(hf == 1, 63 - c, c) * 64 - t * 256
+                diff = lax.broadcasted_iota(jnp.int32, (256, 256), 0) - lax.rem(
+                    lax.broadcasted_iota(jnp.int32, (256, 256), 1), 64)
+                v = jnp.where(diff <= base, v, NEG)
+            ref[score_at(row, ch, 0), :] = v[:, :128]
+            ref[score_at(row, ch, 1), :] = v[:, 128:]
+
+    def values(unit):
+        u, t, hf, ref, row = unit
         shrink = []
         for ch in range(4):
             cs = slice(ch * 256, ch * 256 + 256)
-            s = S[slot, :, cs]
+            v = score_load(ref, row, ch)
             old = top[hf, :, cs]
-            new = jnp.maximum(old, jnp.max(s, axis=0, keepdims=True))
-            p = jnp.exp2(s - new)
+            new = jnp.maximum(old, jnp.max(v, axis=0, keepdims=True))
+            p = jnp.exp2(v - new)
             al = jnp.exp2(old - new)
             top[hf, :, cs] = new
             tot[hf, :, cs] = tot[hf, :, cs] * al + jnp.sum(p, axis=0, keepdims=True)
-            pbb[:, cs] = p.astype(BF16)
+            pbb[u, :, cs] = p.astype(BF16)
             shrink.append(al)
         for ch in range(4):
             cs = slice(ch * 256, ch * 256 + 256)
-            O[hf, :, cs] = O[hf, :, cs] * shrink[ch] + dot(LT[t, :512, :], pbb[:, cs])
+            O[hf, :, cs] = O[hf, :, cs] * shrink[ch] + dot(LT[t, :512, :], pbb[u, :, cs])
+
+    def sibling_arrives(s, line):
+        at = L.at[tile_of(1 - k, line)]
+        remote(at, at, ss.at[s], rs.at[s], c, sib).wait_recv()
 
     for dx in (1, 2, 3):
         x_copy(dx).wait_recv()
     @pl.when(k == 0)
     def _():
-        for dz in (1, 3):
-            z_copy(dz).start()
-
-    def pass_on(s, dz):
+        for dz, part in ((1, 0), (3, 0), (1, 1), (3, 1), (2, 0), (2, 1)):
+            z_copy(dz, part).start()
+
+    def y_start(dz):
         for to in range(2):
             y_copy(dz, to).start()
-        core_copy(s, line_at(dz, 0)).start()
-
-    pass_on(0, 0)
+
+    y_start(0)
+    core_copy(0, t0).start()
 
     @pl.when(k == 1)
     def _():
@@ -213,25 +230,64 @@
             for dx in (1, 3, 2):
                 xb_copy(dz, dx).start()
 
-    @pl.loop(0, 8)
-    def _(s):
+    sibling_arrives(0, t0)
+    LT[t0] = L[t0].T
+    LT[15 - t0] = L[15 - t0].T
+    one, two = units_of(t0)
+    scores(one, False)
+    scores(two, True)
+    values(one)
+    values(two)
+    scores(third, True)
+    values(third)
+
+    def receive(s):
         dz, dy = order(s)
         line = line_at(dz, dy)
 
         @pl.when((s == 1) & (k == 0))
         def _():
-            z_copy(2).start()
+            for dz_ in (1, 3):
+                z_arrive(dz_, 0)
+                y_start(dz_)
+
+        @pl.when((s == 1) & (k == 1))
+        def _():
+            xb_arrive(1)
+            y_start(1)
+
+        @pl.when((s == 2) & (k == 0))
+        def _():
+            z_arrive(1, 1)
+            z_arrive(3, 1)
+
+        @pl.when((s == 2) & (k == 1))
+        def _():
+            xb_arrive(3)
+            y_start(3)
 
         @pl.when(s == 2)
         def _():
-            for at, dz_ in ((2, 1), (3, 3)):
-                wait_line(dz_)
-                pass_on(at, dz_)
+            core_copy(2, line_at(1, 0)).start()
+            core_copy(3, line_at(3, 0)).start()
+
+        @pl.when((s == 3) & (k == 0))
+        def _():
+            z_arrive(2, 0)
+            y_start(2)
+
+        @pl.when((s == 3) & (k == 1))
+        def _():
+            xb_arrive(2)
+            y_start(2)
+
+        @pl.when((s == 4) & (k == 0))
+        def _():
+            z_arrive(2, 1)
 
         @pl.when(s == 4)
         def _():
-            wait_line(2)
-            pass_on(4, 2)
+            core_copy(4, line_at(2, 0)).start()
 
         @pl.when(dy == 1)
         def _():
@@ -240,39 +296,44 @@
                 remote(at, at, sy.at[dz, 0], ry.at[dz, frm], cid(z, 1 - yl, x), frm * 2 + k).wait_recv()
             core_copy(s, line).start()
 
-        @pl.loop(0, 2)
-        def _(kk):
-            @pl.when(kk == 1)
-            def _():
-                at = L.at[tile_of(1 - k, line)]
-                remote(at, at, ss.at[s], rs.at[s], c, sib).wait_recv()
-
-            t = tile_of((k + kk) % 2, line)
-
-            @pl.when(t <= 15 - t0)
-            def _():
-                LT[t] = L[t].astype(F32).T.astype(BF16)
-
-            @pl.loop(0, 2)
-            def _(i):
-                @pl.when(((i == 0) & (t <= 15 - t0)) | ((i == 1) & (t <= t0)))
-                def _():
-                    forward(t, 1 - i)
+    receive(1)
+
+    @pl.loop(1, 8)
+    def _(s):
+        @pl.when(s < 7)
+        def _():
+            receive(s + 1)
+
+        dz, dy = order(s)
+        line = line_at(dz, dy)
+        sibling_arrives(s, line)
+        LT[line] = L[line].T
+
+        @pl.when(line > t0)
+        def _():
+            LT[15 - line] = L[15 - line].T
+
+        one, two = units_of(line)
+        scores(one, False)
+        scores(two, False)
+        values(one)
+        values(two)
 
     for hf in range(2):
         for ch in range(4):
             cs = slice(ch * 256, ch * 256 + 256)
             lse[hf, :, cs] = top[hf, :, cs] + jnp.log2(tot[hf, :, cs])
-            o = O[hf, :, cs] * (1.0 / tot[hf, :, cs])
-            O[hf, :, cs] = o
-            delta[hf, :, cs] = jnp.sum(GT[hf, :, cs].astype(F32) * o, axis=0, keepdims=True)
+            inverse = 1.0 / tot[hf, :, cs]
+            tot[hf, :, cs] = inverse
+            delta[hf, :, cs] = jnp.sum(GT[hf, :, cs].astype(F32) * O[hf, :, cs], axis=0, keepdims=True) * inverse
 
     for d in (1, 2, 3):
         x_copy(d).wait_send()
 
         @pl.when(k == 0)
         def _():
-            z_copy(d).wait_send()
+            z_copy(d, 0).wait_send()
+            z_copy(d, 1).wait_send()
 
         @pl.when(k == 1)
         def _():
@@ -291,20 +352,34 @@
 
         core_copy(s, line_at(dz, dy)).wait_send()
 
-    def backward(t, hf):
-        slot = slot_of(t, hf)
+    def grads(unit):
+        u, t, hf, ref, row = unit
         for ch in range(4):
             cs = slice(ch * 256, ch * 256 + 256)
             dp = dot(L[t, :, :512], GT[hf, :, cs])
-            p = jnp.exp2(S[slot, :, cs] - lse[hf, :, cs])
-            dsb[:, cs] = (p * (dp - delta[hf, :, cs]) * SCALE).astype(BF16)
-            pbb[:, cs] = p.astype(BF16)
+            p = jnp.exp2(score_load(ref, row, ch) - lse[hf, :, cs])
+            dsb[u, :, cs] = (p * (dp - delta[hf, :, cs]) * SCALE).astype(BF16)
+            pbb[u, :, cs] = p.astype(BF16)
+
+    def spread(unit):
+        u, t, hf, ref, row = unit
         for ch in range(4):
             cs = slice(ch * 256, ch * 256 + 256)
-            DA[hf, :, cs] += dot(LT[t], dsb[:, cs])
-        a, b = dot(dsb[...], A[hf]), dot(pbb[...], G[hf])
-        acc[:, :512] += a[:, :512] + b
-        acc[:, 512:] += a[:, 512:]
+            DA[hf, :, cs] += dot(LT[t], dsb[u, :, cs])
+        a, b = dot(dsb[u], A[hf]), dot(pbb[u], G[hf])
+        acc[u, :, :512] = a[:, :512] + b
+        acc[u, :, 512:] = a[:, 512:]
+
+    def pair(line):
+        one, two = units_of(line)
+        grads(one)
+        grads(two)
+        spread(one)
+        spread(two)
+
+        @pl.when(line <= t0)
+        def _():
+            acc[0] += acc[1]
 
     def r1_copy(s, line):
         return remote(L.at[tile_of(1 - k, line)], R1.at[s], s1.at[s], r1.at[s], c, sib)
@@ -387,11 +462,11 @@
 
             @pl.when(line >= t0)
             def _():
-                acc[...] = L[t].astype(F32)
+                acc[0] = L[t].astype(F32)
 
             @pl.when(line < t0)
             def _():
-                acc[...] = jnp.zeros_like(acc)
+                acc[0] = jnp.zeros((256, 576), F32)
 
             for off in (1, 2, 3):
                 @pl.when((z + off) % 4 < z)
@@ -400,48 +475,91 @@
                         slot = ((off - 1) * 2 + dy) * 4 + b
                         at = R2.at[slot]
                         remote(at, at, s2.at[0, 0], r2.at[slot], c, sib).wait_recv()
-                        acc[64 * b:64 * b + 64, :] += at[...].astype(F32)
-
-            L[t] = acc[...].astype(BF16)
+                        acc[0, 64 * b:64 * b + 64, :] += at[...].astype(F32)
+
+            L[t] = acc[0].astype(BF16)
             r3z_each(dy, lambda copy: copy.start())
             if dy == 0:
                 R3[0] = L[t, pl.ds(pl.multiple_of(block_at(x) + 32 * yh, 32), 32), :]
 
-    @pl.loop(0, 8)
+    def send_r1(s, line):
+        @pl.when(active(1 - k, line))
+        def _():
+            r1_copy(s, line).start()
+
+    def merge(s):
+        dz, dy = order(s)
+        line = line_at(dz, dy)
+
+        @pl.when(active(k, line))
+        def _():
+            t = tile_of(k, line)
+            remote(L.at[t], R1.at[s], s1.at[s], r1.at[s], c, sib).wait_recv()
+            L[t] = (L[t].astype(F32) + R1[s].astype(F32)).astype(BF16)
+            r2_each(s, line, lambda copy: copy.start())
+
+    @pl.loop(0, 7)
     def _(i):
         s = 7 - i
         dz, dy = order(s)
         line = line_at(dz, dy)
-
-        @pl.loop(0, 2)
-        def _(kk):
-            kind = (k + 1 - kk) % 2
-            t = tile_of(kind, line)
-
-            @pl.when((kk == 1) & (s < 6) & (k == 0))
-            def _():
-                finish_x(s + 2)
-
-            @pl.when(active(kind, line))
-            def _():
-                acc[...] = jnp.zeros_like(acc)
-
-                @pl.loop(0, 2)
-                def _(i):
-                    @pl.when((i == 0) | (t <= t0))
-                    def _():
-                        backward(t, 1 - i)
-
-                @pl.when(kk == 0)
-                def _():
-                    L[t] = acc[...].astype(BF16)
-                    r1_copy(s, line).start()
-
-                @pl.when(kk == 1)
-                def _():
-                    remote(L.at[t], R1.at[s], s1.at[s], r1.at[s], c, sib).wait_recv()
-                    L[t] = (acc[...] + R1[s].astype(F32)).astype(BF16)
-                    r2_each(s, line, lambda copy: copy.start())
+        pair(line)
+        L[line] = acc[0].astype(BF16)
+
+        @pl.when(line > t0)
+        def _():
+            L[15 - line] = acc[1].astype(BF16)
+
+        send_r1(s, line)
+
+        @pl.when(i > 0)
+        def _():
+            merge(s + 1)
+
+        @pl.when((i > 2) & (k == 0))
+        def _():
+            finish_x(s + 3)
+
+    pair(t0)
+    L[t0] = acc[0].astype(BF16)
+
+    @pl.when(k == 1)
+    def _():
+        send_r1(0, t0)
+
+    grads(third)
+    spread(third)
+    L[15 - t0] = acc[1].astype(BF16)
+
+    @pl.when(k == 0)
+    def _():
+        send_r1(0, t0)
+
+    merge(1)
+
+    def token_rows(i, h):
+        return pl.ds(2048 * i + h, 128, stride=16)
+
+    def by_head(ref, cols, scale=None):
+        both = [ref[hf, :, cols] for hf in range(2)]
+        if scale is not None:
+            both = [both[hf] * scale[hf, :, cols] for hf in range(2)]
+        both = [v.T.astype(BF16) for v in both]
+        return [jnp.concatenate([both[0][r], both[1][r]], axis=0) for r in (slice(0, 64), slice(64, 128))]
+
+    @pl.loop(0, 8)
+    def _(p):
+        o = by_head(O, pl.ds(pl.multiple_of(p * 128, 128), 128), tot)
+        for e in range(2):
+            SA[token_rows(0, 2 * p + e), :] = dot(o[e], wv[2 * p + e])
+
+    merge(0)
+
+    @pl.when(k == 0)
+    def _():
+        finish_x(3)
+        finish_x(2)
+        finish_x(1)
 
     @pl.when(k == 1)
     def _():
@@ -450,27 +568,18 @@
 
     @pl.loop(0, 8)
     def _(p):
-        cols = pl.ds(pl.multiple_of(p * 128, 128), 128)
-        ob = [O[hf, :, cols].T.astype(BF16) for hf in range(2)]
-        db = [DA[hf, :, cols].T.astype(BF16) for hf in range(2)]
+        d = by_head(DA, pl.ds(pl.multiple_of(p * 128, 128), 128))
         for e in range(2):
-            r = slice(64 * e, 64 * e + 64)
-            h = 2 * p + e
-            o = jnp.concatenate([ob[0][r], ob[1][r]], axis=0)
-            d = jnp.concatenate([db[0][r], db[1][r]], axis=0)
-            rows = pl.ds(h, 128, stride=16)
-            X[0, rows, :] = dot(o, wv[h])
-            X[1, rows, :] = dot_nt(d[:, :512], wk[h])
-            qr[h] = d[:, 512:].astype(F32).T.astype(BF16)
-
-        @pl.when((p == 0) & (k == 0))
-        def _():
-            finish_x(1)
-            finish_x(0)
+            SA[token_rows(1, 2 * p + e), :] = dot_nt(d[e][:, :512], wk[2 * p + e])
+            qr[2 * p + e] = d[e][:, 512:].astype(F32).T.astype(BF16)
+
+    @pl.when(k == 0)
+    def _():
+        finish_x(0)
 
     stores = []
-    q[...] = X[0].astype(BF16)
-    og[...] = X[1].astype(BF16)
+    q[...] = SA[0:2048].astype(BF16)
+    og[...] = SA[2048:4096].astype(BF16)
     for i, (ref, out) in enumerate(((q, attn_hbm), (og, gq_hbm), (qr, gqr_hbm))):
         stores.append(pltpu.make_async_copy(ref, out, sout.at[i]))
         stores[i].start()
@@ -534,7 +643,6 @@
     pltpu.VMEM((2048, 128), BF16),
     pltpu.VMEM((16, 128, 512), BF16),
     pltpu.VMEM((16, 512, 128), BF16),
-    pltpu.VMEM((2, 2048, 128), F32),
     DMA((6,)), DMA((4,)),
     pltpu.VMEM((16, 256, 576), BF16),
     pltpu.VMEM((16, 576, 256), BF16),
@@ -542,25 +650,39 @@
     pltpu.VMEM((2, 576, 1024), BF16),
     pltpu.VMEM((2, 1024, 512), BF16),
     pltpu.VMEM((2, 512, 1024), BF16),
-    pltpu.VMEM((17, 256, 1024), F32),
+    pltpu.VMEM((8 * 2048, 128), F32),
+    pltpu.VMEM((9 * 2048, 128), F32),
     pltpu.VMEM((2, 512, 1024), F32),
     pltpu.VMEM((2, 576, 1024), F32),
     pltpu.VMEM((2, 1, 1024), F32),
     pltpu.VMEM((2, 1, 1024), F32),
     pltpu.VMEM((2, 1, 1024), F32),
     pltpu.VMEM((2, 1, 1024), F32),
-    pltpu.VMEM((256, 1024), BF16),
-    pltpu.VMEM((256, 1024), BF16),
-    pltpu.VMEM((256, 576), F32),
+    pltpu.VMEM((2, 256, 1024), BF16),
+    pltpu.VMEM((2, 256, 1024), BF16),
+    pltpu.VMEM((2, 256, 576), F32),
     pltpu.VMEM((8, 256, 576), BF16),
     pltpu.VMEM((24, 64, 576), BF16),
     pltpu.VMEM((8, 64, 576), BF16),
     pltpu.VMEM((16, 32, 576), BF16),
     pltpu.VMEM((128, 576), F32),
     pltpu.VMEM((576, 128), F32),
-    DMA((3,)), DMA((3,)), DMA((3,)), DMA((3,)), DMA((3, 3)), DMA((3, 3)), DMA((4, 2)), DMA((4, 2)), DMA((8,)), DMA((8,)),
+    DMA((3,)), DMA((3,)), DMA((3, 2)), DMA((3, 2)), DMA((3, 3)), DMA((3, 3)), DMA((4, 2)), DMA((4, 2)), DMA((8,)), DMA((8,)),
     DMA((8,)), DMA((8,)), DMA((8, 4)), DMA((24,)), DMA((8, 2)), DMA((16,)), DMA((3,)), DMA((3,)),
 ]
+
+
+def hand_over(*refs):
+    results, outs, held, sems = refs[:4], refs[4:8], refs[8:12], refs[12]
+    loads = [pltpu.make_async_copy(results[i], held[i], sems.at[0, i]) for i in range(4)]
+    stores = [pltpu.make_async_copy(held[i], outs[i], sems.at[1, i]) for i in range(4)]
+    for load in loads:
+        load.start()
+    for load, store in zip(loads, stores):
+        load.wait()
+        store.start()
+    for store in stores:
+        store.wait()
 
 
 def body(q_nope, q_rope, latent, up_keys, up_values, out_grad):
@@ -568,14 +690,15 @@
         return v.reshape(2048, v.shape[2])
 
     hbm = pl.BlockSpec(memory_space=pl.ANY)
-    attn, gq, gqr, gl = pl.pallas_call(
+    shapes = [
+        jax.ShapeDtypeStruct((2048, 128), BF16),
+        jax.ShapeDtypeStruct((2048, 128), BF16),
+        jax.ShapeDtypeStruct((16, 64, 128), BF16),
+        jax.ShapeDtypeStruct((576, 128), F32),
+    ]
+    results = pl.pallas_call(
         kernel,
-        out_shape=[
-            jax.ShapeDtypeStruct((2048, 128), BF16),
-            jax.ShapeDtypeStruct((2048, 128), BF16),
-            jax.ShapeDtypeStruct((16, 64, 128), BF16),
-            jax.ShapeDtypeStruct((576, 128), F32),
-        ],
+        out_shape=shapes,
         in_specs=[hbm] * 6,
         out_specs=[hbm] * 4,
         scratch_shapes=SCRATCH,
@@ -583,6 +706,10 @@
             vmem_limit_bytes=63 * 2**20, collective_id=0, has_side_effects=True),
         cost_estimate=pl.CostEstimate(flops=30_000_000_000, bytes_accessed=12_000_000, transcendentals=9_000_000),
     )(latent.T, flat(q_nope), jnp.transpose(q_rope, (1, 2, 0)), flat(out_grad), up_keys, up_values)
+    attn, gq, gqr, gl = pl.pallas_call(
+        hand_over, out_shape=shapes, in_specs=[hbm] * 4, out_specs=[hbm] * 4,
+        scratch_shapes=[pltpu.VMEM(v.shape, v.dtype) for v in shapes] + [DMA((2, 4))],
+    )(*results)
     return attn.reshape(128, 16, 128), gq.reshape(128, 16, 128), jnp.transpose(gqr, (2, 0, 1)), gl.T
 
 

time: 95.1 us -> 87.3 us (0.918)
  the two profiles are of different devices: /device:TPU:73 before, /device:TPU:1 now
where the time goes in v4:
time: 87.3 us; the launch traced here: 86.2 us
  Pallas kernels  85.6 us (98%)
    pallas_call x1, Pallas kernels, body(): pl.pallas_call(kernel, out_shape=shapes, in_specs=[hbm] * 6, out_specs=[h...  83.3 us
    pallas_call x1, Pallas kernels, body(): pl.pallas_call(hand_over, out_shape=shapes, in_specs=[hbm] * 4, out_specs...  2.26 us

profile of v4, /device:TPU:1, one launch (start us, length us, event | category | flops | bytes accessed | tf_op | source)
XLA Modules:
  0.0 86.2 jit_solution(2413398674337424540)
XLA Ops:
  0.6 83.3 %shard_map.93 = (bf16[2048,128]{1,0:T(8,128)(2,1)}, bf16[2048,128]{1,0:T(8,128)(2,1)}, bf16[16,64,128]{2,1,0:T(8,128)(2,1)}, f32[576,128]{1,0:T(8,128)}) custom-call(bf16[576,128]{1,0:T(8,128)(2,1)} %bitcast.15, bf16[2048,128]{1,0:T(8,128)(2,1)} %bitcast.8, bf16[16,64,128]{2,1,0:T(8,128)(2,1)} %bitcast.13, bf16[2048,128]{1,0:T(8,128)(2,1)} %bitcast.9, ...), custom_call_target="tpu_custom_call" | custom-call | flops 30000001024 | bytes 12000000 | tf_op jit(solution)/shard_map/pallas_call | solution.py:699
  84.0 2.3 %shard_map.94 = (bf16[2048,128]{1,0:T(8,128)(2,1)}, bf16[2048,128]{1,0:T(8,128)(2,1)}, bf16[16,64,128]{2,1,0:T(8,128)(2,1)}, f32[576,128]{1,0:T(8,128)}) custom-call(bf16[2048,128]{1,0:T(8,128)(2,1)} %get-tuple-element.12.refs_0_, bf16[2048,128]{1,0:T(8,128)(2,1)} %get-tuple-element.13.refs_1_, bf16[16,64,128]{2,1,0:T(8,128)(2,1)} %get-tuple-element.14.refs_2_, ...), custom_call_target="tpu_custom_call" | custom-call | tf_op jit(solution)/shard_map/pallas_call | solution.py:709

commit v5 on v4

--- a/solution.py
+++ b/solution.py
@@ -32,7 +32,7 @@
 def kernel(lat_hbm, q_hbm, qr_hbm, og_hbm, wk_hbm, wv_hbm, attn_hbm, gq_hbm, gqr_hbm, gl_hbm,
            lat, q, qr, og, wk, wv, sin, sout,
            L, LT, A, AT, G, GT, SA, SB, O, DA, top, tot, lse, delta, dsb, pbb, acc,
-           R1, R2, R3s, R3, fin, flip,
+           R1, R2, R3s, R3, fin, whole, flip,
            sx, rx, sz, rz, sb, rb, sy, ry, ss, rs, s1, r1, s2, r2, s3, r3, s4, r4):
     c, tp = lax.axis_index("ctx"), lax.axis_index("tp")
     z, yl, x = c // 8, (c // 4) % 2, c % 4
@@ -84,6 +84,9 @@
 
     hello(c, sib)
     hello(c, (1 - yh) * 2 + 1 - k)
+    loads[0].wait()
+    fin[...] = lat[...].astype(F32).T
+    L[mine, pl.ds(block_at(x), 64), :] = fin[pl.ds(pl.multiple_of(64 * k, 64), 64), :].astype(BF16)
     pl.semaphore_wait(barrier, 20)
 
     def x_copy(dx):
@@ -117,9 +120,6 @@
         at = L.at[tile_of(k, line)]
         return remote(at, at, ss.at[s], rs.at[s], c, sib)
 
-    loads[0].wait()
-    fin[...] = lat[...].astype(F32).T
-    L[mine, pl.ds(block_at(x), 64), :] = fin[pl.ds(pl.multiple_of(64 * k, 64), 64), :].astype(BF16)
     for dx in (1, 3, 2):
         x_copy(dx).start()
 
@@ -352,34 +352,26 @@
 
         core_copy(s, line_at(dz, dy)).wait_send()
 
-    def grads(unit):
+    def grads(unit, d):
         u, t, hf, ref, row = unit
         for ch in range(4):
             cs = slice(ch * 256, ch * 256 + 256)
             dp = dot(L[t, :, :512], GT[hf, :, cs])
             p = jnp.exp2(score_load(ref, row, ch) - lse[hf, :, cs])
-            dsb[u, :, cs] = (p * (dp - delta[hf, :, cs]) * SCALE).astype(BF16)
+            dsb[d, :, cs] = (p * (dp - delta[hf, :, cs]) * SCALE).astype(BF16)
             pbb[u, :, cs] = p.astype(BF16)
 
-    def spread(unit):
+    def to_queries(unit, d):
         u, t, hf, ref, row = unit
         for ch in range(4):
             cs = slice(ch * 256, ch * 256 + 256)
-            DA[hf, :, cs] += dot(LT[t], dsb[u, :, cs])
-        a, b = dot(dsb[u], A[hf]), dot(pbb[u], G[hf])
+            DA[hf, :, cs] += dot(LT[t], dsb[d, :, cs])
+
+    def to_keys(unit, d):
+        u, t, hf, ref, row = unit
+        a, b = dot(dsb[d], A[hf]), dot(pbb[u], G[hf])
         acc[u, :, :512] = a[:, :512] + b
         acc[u, :, 512:] = a[:, 512:]
-
-    def pair(line):
-        one, two = units_of(line)
-        grads(one)
-        grads(two)
-        spread(one)
-        spread(two)
-
-        @pl.when(line <= t0)
-        def _():
-            acc[0] += acc[1]
 
     def r1_copy(s, line):
         return remote(L.at[tile_of(1 - k, line)], R1.at[s], s1.at[s], r1.at[s], c, sib)
@@ -503,7 +495,18 @@
         s = 7 - i
         dz, dy = order(s)
         line = line_at(dz, dy)
-        pair(line)
+        one, two = units_of(line)
+        grads(one, 0)
+        grads(two, 1)
+        to_queries(one, 0)
+        to_keys(one, 0)
+        to_queries(two, 1)
+        to_keys(two, 1)
+
+        @pl.when(line < t0)
+        def _():
+            acc[0] += acc[1]
+
         L[line] = acc[0].astype(BF16)
 
         @pl.when(line > t0)
@@ -516,26 +519,57 @@
         def _():
             merge(s + 1)
 
-        @pl.when((i > 2) & (k == 0))
-        def _():
-            finish_x(s + 3)
-
-    pair(t0)
-    L[t0] = acc[0].astype(BF16)
+        @pl.when((i > 3) & (k == 0))
+        def _():
+            finish_x(s + 4)
+
+    one, two = units_of(t0)
+    grads(one, 0)
+    grads(two, 1)
+    to_keys(one, 0)
+    to_keys(two, 1)
+    L[t0] = (acc[0] + acc[1]).astype(BF16)
 
     @pl.when(k == 1)
     def _():
         send_r1(0, t0)
 
-    grads(third)
-    spread(third)
+    merge(1)
+
+    @pl.when(k == 0)
+    def _():
+        finish_x(4)
+
+    @pl.when(k == 1)
+    def _():
+        finish_z(1)
+
+    grads(third, 2)
+    to_keys(third, 2)
     L[15 - t0] = acc[1].astype(BF16)
 
     @pl.when(k == 0)
     def _():
         send_r1(0, t0)
 
-    merge(1)
+    @pl.when(k == 0)
+    def _():
+        merge(0)
+        finish_x(3)
+
+    to_queries(one, 0)
+    to_queries(two, 1)
+    to_queries(third, 2)
+
+    @pl.when(k == 1)
+    def _():
+        merge(0)
+        finish_z(0)
+
+    @pl.when(k == 0)
+    def _():
+        finish_x(2)
+        finish_x(1)
 
     def token_rows(i, h):
         return pl.ds(2048 * i + h, 128, stride=16)
@@ -553,18 +587,9 @@
         for e in range(2):
             SA[token_rows(0, 2 * p + e), :] = dot(o[e], wv[2 * p + e])
 
-    merge(0)
-
     @pl.when(k == 0)
     def _():
-        finish_x(3)
-        finish_x(2)
-        finish_x(1)
-
-    @pl.when(k == 1)
-    def _():
-        finish_z(1)
-        finish_z(0)
+        finish_x(0)
 
     @pl.loop(0, 8)
     def _(p):
@@ -573,10 +598,6 @@
             SA[token_rows(1, 2 * p + e), :] = dot_nt(d[e][:, :512], wk[2 * p + e])
             qr[2 * p + e] = d[e][:, 512:].astype(F32).T.astype(BF16)
 
-    @pl.when(k == 0)
-    def _():
-        finish_x(0)
-
     stores = []
     q[...] = SA[0:2048].astype(BF16)
     og[...] = SA[2048:4096].astype(BF16)
@@ -596,9 +617,10 @@
             fin[my_rows, :] += at[...].astype(F32)
 
     def r4_copy(j):
-        at = fin.at[my_rows, :]
+        at = whole.at[my_rows, :]
         return remote(at, at, s4.at[j - 1], r4.at[j - 1], c, ((yh + j // 2) % 2) * 2 + (k + j % 2) % 2)
 
+    whole[my_rows, :] = fin[my_rows, :].astype(BF16)
     for j in (1, 2, 3):
         r4_copy(j).start()
 
@@ -628,7 +650,7 @@
 
     for j in (1, 2, 3):
         r4_copy(j).wait()
-    flip[...] = fin[...].T
+    flip[...] = whole[...].astype(F32).T
     stores.append(pltpu.make_async_copy(flip, gl_hbm, sout.at[3]))
     stores[3].start()
     for store in stores:
@@ -658,7 +680,7 @@
     pltpu.VMEM((2, 1, 1024), F32),
     pltpu.VMEM((2, 1, 1024), F32),
     pltpu.VMEM((2, 1, 1024), F32),
-    pltpu.VMEM((2, 256, 1024), BF16),
+    pltpu.VMEM((3, 256, 1024), BF16),
     pltpu.VMEM((2, 256, 1024), BF16),
     pltpu.VMEM((2, 256, 576), F32),
     pltpu.VMEM((8, 256, 576), BF16),
@@ -666,6 +688,7 @@
     pltpu.VMEM((8, 64, 576), BF16),
     pltpu.VMEM((16, 32, 576), BF16),
     pltpu.VMEM((128, 576), F32),
+    pltpu.VMEM((128, 576), BF16),
     pltpu.VMEM((576, 128), F32),
     DMA((3,)), DMA((3,)), DMA((3, 2)), DMA((3, 2)), DMA((3, 3)), DMA((3, 3)), DMA((4, 2)), DMA((4, 2)), DMA((8,)), DMA((8,)),
     DMA((8,)), DMA((8,)), DMA((8, 4)), DMA((24,)), DMA((8, 2)), DMA((16,)), DMA((3,)), DMA((3,)),

time: 87.3 us -> 84.9 us (0.973); the launches traced: 86.2 us -> 84.8 us
  Pallas kernels: 85.6 us -> 84 us
    pallas_call x1, Pallas kernels: 83.3 us -> 81.7 us  [body(): pl.pallas_call(kernel, out_shape=shapes, in_specs=[hbm] * 6, out_specs=[h...]
where the time goes in v5:
time: 84.9 us; the launch traced here: 84.8 us
  Pallas kernels  84 us (99%)
    pallas_call x1, Pallas kernels, body(): pl.pallas_call(kernel, out_shape=shapes, in_specs=[hbm] * 6, out_specs=[h...  81.7 us
    pallas_call x1, Pallas kernels, body(): pl.pallas_call(hand_over, out_shape=shapes, in_specs=[hbm] * 4, out_specs...  2.26 us

profile of v5, /device:TPU:1, one launch (start us, length us, event | category | flops | bytes accessed | tf_op | source)
XLA Modules:
  0.0 84.8 jit_solution(2531561913500246596)
XLA Ops:
  0.6 81.7 %shard_map.93 = (bf16[2048,128]{1,0:T(8,128)(2,1)}, bf16[2048,128]{1,0:T(8,128)(2,1)}, bf16[16,64,128]{2,1,0:T(8,128)(2,1)}, f32[576,128]{1,0:T(8,128)}) custom-call(bf16[576,128]{1,0:T(8,128)(2,1)} %bitcast.15, bf16[2048,128]{1,0:T(8,128)(2,1)} %bitcast.8, bf16[16,64,128]{2,1,0:T(8,128)(2,1)} %bitcast.13, bf16[2048,128]{1,0:T(8,128)(2,1)} %bitcast.9, ...), custom_call_target="tpu_custom_call" | custom-call | flops 30000001024 | bytes 12000000 | tf_op jit(solution)/shard_map/pallas_call | solution.py:722
  82.3 2.3 %shard_map.94 = (bf16[2048,128]{1,0:T(8,128)(2,1)}, bf16[2048,128]{1,0:T(8,128)(2,1)}, bf16[16,64,128]{2,1,0:T(8,128)(2,1)}, f32[576,128]{1,0:T(8,128)}) custom-call(bf16[2048,128]{1,0:T(8,128)(2,1)} %get-tuple-element.12.refs_0_, bf16[2048,128]{1,0:T(8,128)(2,1)} %get-tuple-element.13.refs_1_, bf16[16,64,128]{2,1,0:T(8,128)(2,1)} %get-tuple-element.14.refs_2_, ...), custom_call_target="tpu_custom_call" | custom-call | tf_op jit(solution)/shard_map/pallas_call | solution.py:732

commit v6 on v5

--- a/solution.py
+++ b/solution.py
@@ -31,7 +31,7 @@
 
 def kernel(lat_hbm, q_hbm, qr_hbm, og_hbm, wk_hbm, wv_hbm, attn_hbm, gq_hbm, gqr_hbm, gl_hbm,
            lat, q, qr, og, wk, wv, sin, sout,
-           L, LT, A, AT, G, GT, SA, SB, O, DA, top, tot, lse, delta, dsb, pbb, acc,
+           L, LT, AG, AR, AT, GT, SA, SB, O, DA, top, tot, lse, delta, dp2, acc,
            R1, R2, R3s, R3, fin, whole, flip,
            sx, rx, sz, rz, sb, rb, sy, ry, ss, rs, s1, r1, s2, r2, s3, r3, s4, r4):
     c, tp = lax.axis_index("ctx"), lax.axis_index("tp")
@@ -78,16 +78,17 @@
     def _(i):
         hello(cid(z, yl, (x + i) % 4), tp)
 
-    @pl.loop(1, 16)
+    @pl.loop(1, 4)
     def _(i):
-        hello(cid((z + i // 4) % 4, (yl + (i // 2) % 2) % 2, x), ((yh + i % 2) % 2) * 2 + k)
-
+        hello(cid((z + i) % 4, yl, x), tp)
+
+    for to in range(2):
+        hello(cid(z, 1 - yl, x), to * 2 + k)
     hello(c, sib)
-    hello(c, (1 - yh) * 2 + 1 - k)
     loads[0].wait()
     fin[...] = lat[...].astype(F32).T
     L[mine, pl.ds(block_at(x), 64), :] = fin[pl.ds(pl.multiple_of(64 * k, 64), 64), :].astype(BF16)
-    pl.semaphore_wait(barrier, 20)
+    pl.semaphore_wait(barrier, 9)
 
     def x_copy(dx):
         at = L.at[mine, pl.ds(block_at(x), 64), :]
@@ -147,13 +148,13 @@
         for hf in range(2):
             r = slice(64 * hf, 64 * hf + 64)
             blk = jnp.concatenate([pa[r], pb[r]], axis=0)
-            A[hf, cols, :512] = blk.astype(BF16)
+            AG[hf, cols, :] = blk.astype(BF16)
             AT[hf, :512, cols] = blk.T.astype(BF16)
             rblk = jnp.concatenate([ra[r], rb[r]], axis=0)
-            A[hf, cols, 512:] = rblk.astype(BF16)
+            AR[hf, cols, :] = rblk.astype(BF16)
             AT[hf, 512:, cols] = rblk.T.astype(BF16)
             gblk = jnp.concatenate([ga[r], gb[r]], axis=0)
-            G[hf, cols, :] = gblk.astype(BF16)
+            AG[hf, pl.ds(pl.multiple_of(1024 + p * 128, 128), 128), :] = gblk.astype(BF16)
             GT[hf, :, cols] = gblk.T.astype(BF16)
 
     top[...] = jnp.full_like(top, NEG)
@@ -199,11 +200,11 @@
             al = jnp.exp2(old - new)
             top[hf, :, cs] = new
             tot[hf, :, cs] = tot[hf, :, cs] * al + jnp.sum(p, axis=0, keepdims=True)
-            pbb[u, :, cs] = p.astype(BF16)
+            dp2[u, :, 1024 + ch * 256:1280 + ch * 256] = p.astype(BF16)
             shrink.append(al)
         for ch in range(4):
             cs = slice(ch * 256, ch * 256 + 256)
-            O[hf, :, cs] = O[hf, :, cs] * shrink[ch] + dot(LT[t, :512, :], pbb[u, :, cs])
+            O[hf, :, cs] = O[hf, :, cs] * shrink[ch] + dot(LT[t, :512, :], dp2[u, :, 1024 + ch * 256:1280 + ch * 256])
 
     def sibling_arrives(s, line):
         at = L.at[tile_of(1 - k, line)]
@@ -358,20 +359,19 @@
             cs = slice(ch * 256, ch * 256 + 256)
             dp = dot(L[t, :, :512], GT[hf, :, cs])
             p = jnp.exp2(score_load(ref, row, ch) - lse[hf, :, cs])
-            dsb[d, :, cs] = (p * (dp - delta[hf, :, cs]) * SCALE).astype(BF16)
-            pbb[u, :, cs] = p.astype(BF16)
+            dp2[d, :, cs] = (p * (dp - delta[hf, :, cs]) * SCALE).astype(BF16)
+            dp2[d, :, 1024 + ch * 256:1280 + ch * 256] = p.astype(BF16)
 
     def to_queries(unit, d):
         u, t, hf, ref, row = unit
         for ch in range(4):
             cs = slice(ch * 256, ch * 256 + 256)
-            DA[hf, :, cs] += dot(LT[t], dsb[d, :, cs])
+            DA[hf, :, cs] += dot(LT[t], dp2[d, :, cs])
 
     def to_keys(unit, d):
         u, t, hf, ref, row = unit
-        a, b = dot(dsb[d], A[hf]), dot(pbb[u], G[hf])
-        acc[u, :, :512] = a[:, :512] + b
-        acc[u, :, 512:] = a[:, 512:]
+        acc[u, :, :512] = dot(dp2[d], AG[hf])
+        acc[u, :, 512:] = dot(dp2[d, :, :1024], AR[hf])
 
     def r1_copy(s, line):
         return remote(L.at[tile_of(1 - k, line)], R1.at[s], s1.at[s], r1.at[s], c, sib)
@@ -668,9 +668,9 @@
     DMA((6,)), DMA((4,)),
     pltpu.VMEM((16, 256, 576), BF16),
     pltpu.VMEM((16, 576, 256), BF16),
-    pltpu.VMEM((2, 1024, 576), BF16),
+    pltpu.VMEM((2, 2048, 512), BF16),
+    pltpu.VMEM((2, 1024, 64), BF16),
     pltpu.VMEM((2, 576, 1024), BF16),
-    pltpu.VMEM((2, 1024, 512), BF16),
     pltpu.VMEM((2, 512, 1024), BF16),
     pltpu.VMEM((8 * 2048, 128), F32),
     pltpu.VMEM((9 * 2048, 128), F32),
@@ -680,8 +680,7 @@
     pltpu.VMEM((2, 1, 1024), F32),
     pltpu.VMEM((2, 1, 1024), F32),
     pltpu.VMEM((2, 1, 1024), F32),
-    pltpu.VMEM((3, 256, 1024), BF16),
-    pltpu.VMEM((2, 256, 1024), BF16),
+    pltpu.VMEM((3, 256, 2048), BF16),
     pltpu.VMEM((2, 256, 576), F32),
     pltpu.VMEM((8, 256, 576), BF16),
     pltpu.VMEM((24, 64, 576), BF16),

time: 84.9 us -> 85.9 us (1.012)
  Pallas kernels: 84 us -> 85 us
    pallas_call x1, Pallas kernels: 81.7 us -> 82.7 us  [body(): pl.pallas_call(kernel, out_shape=shapes, in_specs=[hbm] * 6, out_specs=[h...]
where the time goes in v6:
time: 85.9 us; the launch traced here: 85.8 us
  Pallas kernels  85 us (99%)
    pallas_call x1, Pallas kernels, body(): pl.pallas_call(kernel, out_shape=shapes, in_specs=[hbm] * 6, out_specs=[h...  82.7 us
    pallas_call x1, Pallas kernels, body(): pl.pallas_call(hand_over, out_shape=shapes, in_specs=[hbm] * 4, out_specs...  2.26 us

profile of v6, /device:TPU:1, one launch (start us, length us, event | category | flops | bytes accessed | tf_op | source)
XLA Modules:
  0.0 85.8 jit_solution(12128257287409617914)
XLA Ops:
  0.6 82.7 %shard_map.93 = (bf16[2048,128]{1,0:T(8,128)(2,1)}, bf16[2048,128]{1,0:T(8,128)(2,1)}, bf16[16,64,128]{2,1,0:T(8,128)(2,1)}, f32[576,128]{1,0:T(8,128)}) custom-call(bf16[576,128]{1,0:T(8,128)(2,1)} %bitcast.15, bf16[2048,128]{1,0:T(8,128)(2,1)} %bitcast.8, bf16[16,64,128]{2,1,0:T(8,128)(2,1)} %bitcast.13, bf16[2048,128]{1,0:T(8,128)(2,1)} %bitcast.9, ...), custom_call_target="tpu_custom_call" | custom-call | flops 30000001024 | bytes 12000000 | tf_op jit(solution)/shard_map/pallas_call | solution.py:721
  83.3 2.3 %shard_map.94 = (bf16[2048,128]{1,0:T(8,128)(2,1)}, bf16[2048,128]{1,0:T(8,128)(2,1)}, bf16[16,64,128]{2,1,0:T(8,128)(2,1)}, f32[576,128]{1,0:T(8,128)}) custom-call(bf16[2048,128]{1,0:T(8,128)(2,1)} %get-tuple-element.12.refs_0_, bf16[2048,128]{1,0:T(8,128)(2,1)} %get-tuple-element.13.refs_1_, bf16[16,64,128]{2,1,0:T(8,128)(2,1)} %get-tuple-element.14.refs_2_, ...), custom_call_target="tpu_custom_call" | custom-call | tf_op jit(solution)/shard_map/pallas_call | solution.py:731
